TPU v7x, 512 devices: a whole 4x8x8 slice. The times are simulated.
512 devices in a mesh: tm: 64 (over y, x, core), rows: 8 (over z).
Axes of the slice: x: 4, y: 8, z: 8, core: 2. Of those that a mesh axis runs over, the one named last changes fastest.
Arguments:
- latents: bfloat16 [256, 8, 32, 384], P('tm', 'rows'), may hold values from -16 to 16
- gain_one: float32 [384], replicated, may hold values from 0.1 to 1.9
- conv_weight: bfloat16 [27, 384, 384], P(None, None, 'tm'), may hold values from -0.0625 to 0.0625
- gain_two: float32 [384], replicated, may hold values from 0.1 to 1.9
- qkv_weight: bfloat16 [3, 384, 384], P(None, None, 'tm'), may hold values from -3 to 3
- out_weight: bfloat16 [384, 384], P(None, 'tm'), may hold values from -0.3125 to 0.3125
Outputs:
- block_out: bfloat16 [256, 8, 32, 384], P('tm', 'rows')
All inputs are finite; a program needn't handle non-finite values.
Results may differ from a plain program's by a relative error of at most 0.0059.
Values may be sent and summed in bfloat16 or wider, within the bound.
A program may use at most 128 MiB of HBM per device.

v0:
```python
import jax
import jax.numpy as jnp
from jax import lax
from jax.sharding import PartitionSpec as P

GROUPS = 32


def passed_along(value, axis, steps):
    count = lax.axis_size(axis)
    first, last = (max(0, -steps), min(count, count - steps))
    return lax.ppermute(value, axis, [(source, source + steps) for source in range(first, last)])


def with_halo(cells, sides, width):
    for axis, dim in sides:
        count = lax.axis_size(axis)
        ends = count - 1
        head = lax.slice_in_dim(cells, 0, width, axis=dim)
        tail = lax.slice_in_dim(cells, cells.shape[dim] - width, cells.shape[dim], axis=dim)
        cells = jnp.concatenate(
            [
                lax.ppermute(tail, axis, [(i, (i + 1) % count) for i in range(ends)]),
                cells,
                lax.ppermute(head, axis, [((i + 1) % count, i) for i in range(ends)]),
            ],
            axis=dim,
        )
    return cells


def group_norm(field, scaling):
    nframes, nrows, ncols, nchan = field.shape
    grouped = field.reshape(nframes, nrows * ncols, GROUPS, nchan // GROUPS)
    sample_count = nrows * ncols * (nchan // GROUPS) * lax.axis_size("rows")
    summed = lax.psum(jnp.sum(grouped, axis=(1, 3)), "rows")
    average = summed / sample_count
    deviation = grouped - average[:, None, :, None]
    variance = lax.psum(jnp.sum(deviation * deviation, axis=(1, 3)), "rows") / sample_count
    normed_out = (grouped - average[:, None, :, None]) * lax.rsqrt(
        variance[:, None, :, None] + 1e-06
    )
    return normed_out.reshape(field.shape) * scaling


def body(latents, gain_one, conv_weight, gain_two, qkv_weight, out_weight):
    nframes, tile_rows, columns, channels = latents.shape
    activated = jax.nn.silu(group_norm(latents.astype(jnp.float32), gain_one)).astype(jnp.bfloat16)
    earlier = passed_along(activated[nframes - 2 :], "tm", 1)
    extended = jnp.concatenate([earlier, activated], 0)
    rimmed = with_halo(extended, (("rows", 1),), 1)
    padded = jnp.pad(rimmed, ((0, 0), (0, 0), (1, 1), (0, 0)))
    positions = nframes * tile_rows * columns
    block_piece = lax.all_gather(conv_weight, "tm", axis=2, tiled=True)
    running = jnp.zeros((positions, block_piece.shape[2]), jnp.float32)
    for tap_index in range(27):
        tap_time = tap_index // 9
        tap_row = tap_index // 3 % 3
        tap_col = tap_index % 3
        running = running + jnp.dot(
            padded[
                tap_time : tap_time + nframes,
                tap_row : tap_row + tile_rows,
                tap_col : tap_col + columns,
            ].reshape(positions, channels),
            block_piece[tap_index],
            preferred_element_type=jnp.float32,
        )
    through = (latents.astype(jnp.float32) + running.reshape(latents.shape)).astype(jnp.bfloat16)
    normed = (
        group_norm(through.astype(jnp.float32), gain_two)
        .astype(jnp.bfloat16)
        .reshape(positions, channels)
    )
    full_qkv, full_out = (
        lax.all_gather(qkv_weight, "tm", axis=2, tiled=True),
        lax.all_gather(out_weight, "tm", axis=1, tiled=True),
    )
    per_frame = tile_rows * columns
    queries = (
        jnp.dot(normed, full_qkv[0], preferred_element_type=jnp.float32)
        .astype(jnp.bfloat16)
        .reshape(nframes, per_frame, channels)
    )
    key_rows = (
        jnp.dot(normed, full_qkv[1], preferred_element_type=jnp.float32)
        .astype(jnp.bfloat16)
        .reshape(nframes, per_frame, channels)
    )
    value_rows = (
        jnp.dot(normed, full_qkv[2], preferred_element_type=jnp.float32)
        .astype(jnp.bfloat16)
        .reshape(nframes, per_frame, channels)
    )
    score_scale = channels ** (-0.5)
    running_max = jnp.full((nframes, per_frame), -jnp.inf, jnp.float32)
    norm_sum = jnp.zeros((nframes, per_frame), jnp.float32)
    accum = jnp.zeros((nframes, per_frame, channels), jnp.float32)
    key_piece = lax.all_gather(key_rows, "rows", axis=1, tiled=True)
    value_piece = lax.all_gather(value_rows, "rows", axis=1, tiled=True)
    scores = (
        jnp.einsum("fqc,fkc->fqk", queries, key_piece, preferred_element_type=jnp.float32)
        * score_scale
    )
    new_max = jnp.max(scores, axis=2)
    correction = jnp.exp(running_max - new_max)
    expon = jnp.exp(scores - new_max[:, :, None])
    norm_sum = norm_sum * correction + jnp.sum(expon, axis=2)
    update = jnp.einsum(
        "fqk,fkc->fqc", expon.astype(jnp.bfloat16), value_piece, preferred_element_type=jnp.float32
    )
    accum = accum * correction[:, :, None] + update
    final_max, norm_sum, accum = (new_max, norm_sum, accum)
    attended = (accum / norm_sum[:, :, None]).astype(jnp.bfloat16).reshape(positions, channels)
    result = through.astype(jnp.float32).reshape(positions, channels) + jnp.dot(
        attended, full_out, preferred_element_type=jnp.float32
    )
    return result.astype(jnp.bfloat16).reshape(latents.shape)


def solution(mesh):
    in_specs = (
        P("tm", "rows", None, None),
        P(),
        P(None, None, "tm"),
        P(),
        P(None, None, "tm"),
        P(None, "tm"),
    )
    out_specs = P("tm", "rows", None, None)
    return jax.shard_map(body, mesh=mesh, in_specs=in_specs, out_specs=out_specs, check_vma=False)
```

profile of v0, /device:TPU:2, one launch (start us, length us, event | category | flops | bytes accessed | tf_op | source)
XLA Modules:
  0.0 365.2 jit_solution(15415483101310784391)
XLA Ops:
  6.5 0.7 all-gather.3.cloned.1.call-update
  7.3 0.9 convert_reduce_fusion
  8.4 23.2 %psum.28 = f32[4,32]{1,0:T(4,128)S(1)} all-reduce(f32[4,32]{1,0:T(4,128)S(1)} %reduce_sum.59), channel_id=1, replica_groups=mesh['tm'=64,'rows'=8] {'rows'}, use_global_device_ids=true, to_apply=%region_2.0 | all-reduce | flops 128 | bytes 1024 | tf_op jit(solution)/shard_map/psum | solution.py:36
  31.8 0.9 fusion.50
  32.9 14.2 %psum.29 = f32[4,32]{1,0:T(4,128)S(1)} all-reduce(f32[4,32]{1,0:T(4,128)S(1)} %reduce_sum.62), channel_id=1, replica_groups=mesh['tm'=64,'rows'=8] {'rows'}, use_global_device_ids=true, to_apply=%region_5.6 | all-reduce | flops 128 | bytes 1024 | tf_op jit(solution)/shard_map/psum | solution.py:39
  47.3 1.0 fusion.57
  48.3 1.9 collective-permute-start
  50.3 50.8 %all_gather.16 = bf16[3,384,384]{1,0,2:T(4,128)(2,1)S(1)} all-gather(bf16[3,384,6]{1,0,2:T(4,128)(2,1)S(1)} %copy.70), channel_id=1, replica_groups=mesh['tm'=64,'rows'=8] {'tm'}, dimensions={2}, use_global_device_ids=true | all-gather | bytes 898560 | tf_op jit(solution)/shard_map/all_gather | solution.py:76
  101.1 1.2 fusion.69
  102.4 3.8 %collective-permute-start.1 = (bf16[6,1,32,384]{3,2,1,0:T(8,128)(2,1)S(1)}, bf16[6,1,32,384]{3,2,1,0:T(8,128)(2,1)S(1)}, u32[]{:S(2)}, u32[]{:S(2)}) collective-permute-start(bf16[6,1,32,384]{3,2,1,0:T(8,128)(2,1)S(1)} %pad_maximum_fusion), channel_id=1, source_target_pairs={{0,1},{1,2},{2,3},{3,4},{4,5},{5,6},{6,7},{8,9},{9,10},{10,11},{11... | collective-permute-start | bytes 442376 | tf_op jit(solution)/shard_map/ppermute | solution.py:23
  106.2 1.3 collective-permute-start.2
  107.5 46.5 %all-gather = bf16[64,6,384]{2,1,0:T(8,128)(2,1)S(1)} all-gather(bf16[1,6,384]{2,1,0:T(8,128)(2,1)S(1)} %bitcast.208), channel_id=1, replica_groups=mesh['tm'=64,'rows'=8] {'tm'}, dimensions={0}, use_global_device_ids=true | all-gather | bytes 299520 | tf_op jit(solution)/shard_map/all_gather | solution.py:77
  154.0 1.8 copy.103
  155.8 1.8 copy.102
  157.6 1.8 copy.104
  159.4 0.8 reshape.193
  160.2 0.7 fusion.62
  161.1 0.7 fusion.72
  161.8 0.7 fusion.71
  162.5 1.1 fusion.70
  163.7 11.6 %fusion.68 = (bf16[1,384,384]{1,0,2:T(2,128)(2,1)S(1)}, bf16[1,384,384]{1,0,2:T(2,128)(2,1)S(1)}, bf16[1,384,384]{1,0,2:T(2,128)(2,1)S(1)}, bf16[1,384,384]{1,0,...) fusion(bf16[27,384,384]{1,0,2:T(8,128)(2,1)} %all-gather.3.clon, ...), kind=kLoop, calls=%fused_computation.114 | loop fusion | bytes 4718592 | tf_op jit(solution)/shard_map/slice | solution.py:66
  175.3 2.8 copy.75
  178.1 2.8 copy.76
  180.9 2.8 copy.77
  183.6 1.8 copy.78
  185.4 1.8 copy.79
  187.2 1.8 copy.80
  189.0 1.8 copy.81
  190.8 23.2 %fusion.67 = (bf16[1,384,384]{1,0,2:T(2,128)(2,1)S(1)}, bf16[1,384,384]{1,0,2:T(2,128)(2,1)S(1)}, bf16[1,384,384]{1,0,2:T(2,128)(2,1)S(1)}, bf16[1,384,384]{1,0,...) fusion(bf16[27,384,384]{1,0,2:T(8,128)(2,1)} %all-gather.3.clon, ...), kind=kLoop, calls=%fused_computation.113 | loop fusion | bytes 11206656 | tf_op jit(solution)/shard_map/slice | solution.py:66
  214.0 2.8 copy.83
  216.8 2.8 copy.82
  219.5 2.8 copy.84
  222.3 2.8 copy.86
  225.0 2.8 copy.85
  227.8 2.8 copy.87
  230.6 2.8 copy.88
  233.3 2.8 copy.89
  236.1 2.8 copy.90
  238.9 2.8 copy.92
  241.6 2.8 copy.91
  244.4 2.8 copy.93
  247.2 2.8 copy.95
  249.9 2.8 copy.94
  252.7 2.8 copy.96
  255.5 0.8 copy.97
  256.3 0.9 copy.98
  257.2 0.9 copy.99
  258.1 0.9 copy.101
  258.9 1.1 copy.100
  260.1 1.2 fusion.46
  261.2 1.1 fusion.37
  262.4 1.1 fusion.33
  266.4 0.2 fusion.4
  267.4 0.3 copy-done.12
  268.4 0.3 copy-done.8
  269.5 0.3 copy-done.22
  271.4 0.3 convert_reduce_fusion.1
  271.9 16.8 %psum.30 = f32[4,32]{1,0:T(4,128)S(1)} all-reduce(f32[4,32]{1,0:T(4,128)S(1)} %reduce_sum.81), channel_id=1, replica_groups=mesh['tm'=64,'rows'=8] {'rows'}, use_global_device_ids=true, to_apply=%region_8.9 | all-reduce | flops 128 | bytes 1024 | tf_op jit(solution)/shard_map/psum | solution.py:36
  289.1 14.2 %psum.31 = f32[4,32]{1,0:T(4,128)S(1)} all-reduce(f32[4,32]{1,0:T(4,128)S(1)} %reduce_sum.84), channel_id=1, replica_groups=mesh['tm'=64,'rows'=8] {'rows'}, use_global_device_ids=true, to_apply=%region_11.12 | all-reduce | flops 128 | bytes 1024 | tf_op jit(solution)/shard_map/psum | solution.py:39
  303.8 26.4 %all_gather.17 = bf16[4,256,384]{2,1,0:T(8,128)(2,1)S(1)} all-gather(bf16[4,32,384]{2,1,0:T(8,128)(2,1)S(1)} %bitcast.200), channel_id=1, replica_groups=mesh['tm'=64,'rows'=8] {'rows'}, dimensions={1}, use_global_device_ids=true | all-gather | bytes 884736 | tf_op jit(solution)/shard_map/all_gather | solution.py:99
  330.4 0.4 fusion.73
  331.3 25.9 %all_gather.18 = bf16[4,256,384]{2,1,0:T(8,128)(2,1)S(1)} all-gather(bf16[4,32,384]{2,1,0:T(8,128)(2,1)S(1)} %bitcast.199), channel_id=1, replica_groups=mesh['tm'=64,'rows'=8] {'rows'}, dimensions={1}, use_global_device_ids=true | all-gather | bytes 884736 | tf_op jit(solution)/shard_map/all_gather | solution.py:100
  357.1 0.3 fusion.6
  357.5 0.9 fusion.7
  (157 shorter events, 9.1 us)
Async XLA Ops:
  6.5 43.7 %copy-start.48 = (bf16[3,384,6]{1,2,0:T(8,128)(2,1)S(1)}, bf16[3,384,6]{1,2,0:T(8,128)(2,1)}, u32[]{:S(2)}) copy-start(bf16[3,384,6]{1,2,0:T(8,128)(2,1)} %param.10) | copy-start | bytes 41476
  6.5 157.2 %all-gather.3.cloned.1.call-start = ((), (), s32[]{:S(2)}) async-start(), calls=%async_computation | async-start | bytes 9584640 | tf_op jit(solution)/shard_map/all_gather | solution.py:54
  48.3 54.0 %collective-permute-start = (bf16[2,1,32,384]{3,2,1,0:T(8,128)(2,1)S(1)}, bf16[2,1,32,384]{3,2,1,0:T(8,128)(2,1)S(1)}, u32[]{:S(2)}, u32[]{:S(2)}) collective-permute-start(bf16[2,1,32,384]{3,2,1,0:T(8,128)(2,1)S(1)} %slice.247), channel_id=1, source_target_pairs={{0,8},{8,16},{16,24},{24,32},{32,40},{40,48},{48,56},{56,64},{64,7... | collective-permute-start | bytes 147464 | tf_op jit(solution)/shard_map/ppermute | solution.py:12
  101.1 6.4 %copy-start.49 = (bf16[384,6]{0,1:T(8,128)(2,1)S(1)}, bf16[384,6]{0,1:T(8,128)(2,1)}, u32[]{:S(2)}) copy-start(bf16[384,6]{0,1:T(8,128)(2,1)} %param.11) | copy-start | bytes 13828
  102.4 58.5 %collective-permute-start.1 = (bf16[6,1,32,384]{3,2,1,0:T(8,128)(2,1)S(1)}, bf16[6,1,32,384]{3,2,1,0:T(8,128)(2,1)S(1)}, u32[]{:S(2)}, u32[]{:S(2)}) collective-permute-start(bf16[6,1,32,384]{3,2,1,0:T(8,128)(2,1)S(1)} %pad_maximum_fusion), channel_id=1, source_target_pairs={{0,1},{1,2},{2,3},{3,4},{4,5},{5,6},{6,7},{8,9},{9,10},{10,11},{11... | collective-permute-start | bytes 442376 | tf_op jit(solution)/shard_map/ppermute | solution.py:23
  106.2 54.7 %collective-permute-start.2 = (bf16[6,1,32,384]{3,2,1,0:T(8,128)(2,1)S(1)}, bf16[6,1,32,384]{3,2,1,0:T(8,128)(2,1)S(1)}, u32[]{:S(2)}, u32[]{:S(2)}) collective-permute-start(bf16[6,1,32,384]{3,2,1,0:T(8,128)(2,1)S(1)} %pad_maximum_fusion), channel_id=1, source_target_pairs={{1,0},{2,1},{3,2},{4,3},{5,4},{6,5},{7,6},{9,8},{10,9},{11,10},{12... | collective-permute-start | bytes 442376 | tf_op jit(solution)/shard_map/ppermute | solution.py:25
  258.0 2.0 copy-start.17
  258.0 3.2 copy-start.18
  258.9 3.5 copy-start.19
  260.0 3.6 copy-start.20
  260.0 3.6 copy-start.39
  260.0 3.8 %copy-start.21 = (bf16[1,384,384]{2,1,0:T(8,128)(2,1)S(1)}, bf16[1,384,384]{2,1,0:T(8,128)(2,1)}, u32[]{:S(2)}) copy-start(bf16[1,384,384]{2,1,0:T(8,128)(2,1)} %copy.95) | copy-start | bytes 884740
  260.0 3.8 %copy-start.38 = (bf16[4,1,32,384]{3,2,1,0:T(8,128)(2,1)S(1)}, bf16[4,1,32,384]{3,2,1,0:T(8,128)(2,1)}, u32[]{:S(2)}) copy-start(bf16[4,1,32,384]{3,2,1,0:T(8,128)(2,1)} %get-tuple-element.40) | copy-start | bytes 294916
  261.2 2.9 copy-start.37
  262.4 1.9 copy-start.9
  262.4 1.9 copy-start.40
  263.8 1.0 copy-start.7
  263.8 1.0 copy-start.36
  264.1 1.0 copy-start.6
  264.1 1.0 copy-start.35
  264.3 1.0 copy-start.4
  264.3 1.0 copy-start.42
  264.8 1.0 copy-start.3
  264.8 1.0 copy-start.34
  265.1 1.0 copy-start.1
  265.1 1.0 copy-start.33
  265.4 1.0 copy-start.25
  265.4 1.0 copy-start.47
  265.8 1.0 copy-start.13
  265.8 1.0 copy-start.32
  266.1 1.0 copy-start.24
  266.1 1.0 copy-start.46
  266.6 1.0 copy-start.12
  266.7 1.0 copy-start.31
  266.9 1.0 copy-start.11
  266.9 1.0 copy-start.41
  267.2 1.0 copy-start.10
  267.2 1.0 copy-start.30
  267.7 1.0 copy-start.8
  267.7 1.0 copy-start.29
  267.9 1.0 copy-start.23
  267.9 1.0 copy-start.45
  268.2 1.0 copy-start.5
  268.2 1.0 copy-start.28
  268.7 1.0 copy-start.22
  268.7 1.0 copy-start.44
  269.2 1.0 copy-start.2
  269.2 1.0 copy-start.27
  270.4 0.9 copy-start
  270.4 0.9 copy-start.43
  270.9 32.6 %copy-start.50 = (f32[384]{0:T(512)S(1)}, f32[384]{0:T(512)}, u32[]{:S(2)}) copy-start(f32[384]{0:T(512)} %param.9) | copy-start | bytes 4612
  271.1 32.4 %copy-start.16 = (bf16[1,384,384]{2,1,0:T(8,128)(2,1)S(1)}, bf16[1,384,384]{2,1,0:T(8,128)(2,1)}, u32[]{:S(2)}) copy-start(bf16[1,384,384]{2,1,0:T(8,128)(2,1)} %copy.103) | copy-start | bytes 884740
  271.7 58.5 %copy-start.15 = (bf16[1,384,384]{2,1,0:T(8,128)(2,1)S(1)}, bf16[1,384,384]{2,1,0:T(8,128)(2,1)}, u32[]{:S(2)}) copy-start(bf16[1,384,384]{2,1,0:T(8,128)(2,1)} %copy.102) | copy-start | bytes 884740
  303.8 27.3 %copy-start.14 = (bf16[1,384,384]{2,1,0:T(8,128)(2,1)S(1)}, bf16[1,384,384]{2,1,0:T(8,128)(2,1)}, u32[]{:S(2)}) copy-start(bf16[1,384,384]{2,1,0:T(8,128)(2,1)} %copy.104) | copy-start | bytes 884740
  331.3 26.2 %copy-start.26 = (bf16[384,384]{1,0:T(8,128)(2,1)S(1)}, bf16[384,384]{1,0:T(8,128)(2,1)}, u32[]{:S(2)}) copy-start(bf16[384,384]{1,0:T(8,128)(2,1)} %reshape.193) | copy-start | bytes 884740
Sparse Core Ops, SparseCore 0:
  10.7 94.7 all-gather.2
where the time goes:
time: 367 us; the launch traced here: 365 us
  blocking collectives  218 us (59%)
  local copies, waits for them, and re-layouts  110 us (30%)
  between operations  14.3 us (4%)
  matrix products  10.7 us (3%)
  starting transfers between devices  7.05 us (2%)
  other arithmetic  4.42 us (1%)
    unnamed x134, local copies, waits for them, and re-layouts  70.2 us
    all_gather x1, blocking collectives, body(): lax.all_gather(qkv_weight, 'tm', axis=2, tiled=True)  50.8 us
    all_gather x1, blocking collectives, body(): lax.all_gather(out_weight, 'tm', axis=1, tiled=True)  46.5 us
    psum x2, blocking collectives, group_norm(): summed = lax.psum(jnp.sum(grouped, axis=(1, 3)), 'rows')  40 us
    slice x2, local copies, waits for them, and re-layouts, body(): block_piece[tap_index]  34.8 us
    psum x2, blocking collectives, group_norm(): lax.psum(jnp.sum(deviation * deviation, axis=(1, 3)), 'rows') / sample_count  28.3 us
    all_gather x1, blocking collectives, body(): key_piece = lax.all_gather(key_rows, 'rows', axis=1, tiled=True)  26.4 us
    all_gather x1, blocking collectives, body(): value_piece = lax.all_gather(value_rows, 'rows', axis=1, tiled=True)  25.9 us
  transfers between devices with their start and end apart: 4, of which 0 were waited for; matrix products, arithmetic and copies ran while one was open for 4% of the time, Pallas kernels for 0%

commit v1 on v0

v1 whole, which is shorter than its diff:
```python
import jax
import jax.numpy as jnp
from jax import lax
from jax.experimental import pallas as pl
from jax.experimental.pallas import tpu as pltpu
from jax.sharding import PartitionSpec as P

C = 384
NX, NY, NZ = 4, 8, 8
BF = jnp.bfloat16
F32 = jnp.float32
MESH = pl.DeviceIdType.MESH
NSEND = 96


def iota(shape, dim):
    return lax.broadcasted_iota(jnp.int32, shape, dim)


def twelfth(i):
    return (i * 43691) >> 19


def one_hot(mask):
    return jnp.where(mask, 1.0, 0.0).astype(BF)


def dot_nn(a, b):
    return lax.dot_general(a, b, (((1,), (0,)), ((), ())), preferred_element_type=F32)


def dot_nt(a, b):
    return lax.dot_general(a, b, (((1,), (1,)), ((), ())), preferred_element_type=F32)


def group_means(sums, gmat):
    rows = iota((16, C), 0)
    stack = jnp.zeros((16, C), F32)
    for n, s in enumerate(sums):
        high = s.astype(BF).astype(F32)
        rest = s - high
        mid = rest.astype(BF).astype(F32)
        for k, part in enumerate((high, mid, rest - mid)):
            stack = jnp.where(rows == 3 * n + k, part, stack)
    res = dot_nn(stack.astype(BF), gmat)
    out = []
    for n in range(len(sums)):
        total = res[3 * n : 3 * n + 1] + res[3 * n + 1 : 3 * n + 2] + res[3 * n + 2 : 3 * n + 3]
        out.append(total * (1.0 / (12 * 256)))
    return out


def kernel(
    lat_in, wc_in, wq_in, gain1, gain2, out_ref,
    lat, sibc, sibq, wall, wq, act, acc, thr_s, thr, thrn, obuf, gmat,
    sends, lat_sem, sibw_sem, yp, ym, xp, xm, xpp, xmm, ssib, qx, qy, qsib, exsem, outsem,
):
    tm = lax.axis_index("tm")
    z = lax.axis_index("rows")
    c = lax.rem(tm, 2)
    q = tm // 2
    x = lax.rem(q, NX)
    y = q // NX
    g = z // 4
    zc = lax.rem(z, 4)
    half = zc // 2
    fsel = lax.rem(zc, 2)

    pending = []

    def place(yy, xx, core):
        return (lax.rem(yy + NY, NY) * NX + lax.rem(xx + NX, NX)) * 2 + core

    def send(src, dst, rsem, to_tm, to_z, when=None):
        d = pltpu.make_async_remote_copy(
            src_ref=src, dst_ref=dst, send_sem=sends.at[len(pending)], recv_sem=rsem,
            device_id=(to_tm, to_z), device_id_type=MESH,
        )
        if when is None:
            d.start()
        else:
            pl.when(when)(d.start)
        pending.append((when, d))

    def send_or_keep(src, dst, rsem, to_tm, to_z):
        here = jnp.logical_and(to_tm == tm, to_z == z)
        send(src, dst, rsem, to_tm, to_z, jnp.logical_not(here))
        pl.when(here)(pltpu.make_async_copy(src, dst, rsem).start)

    def arrived(ref, sem):
        pltpu.make_async_copy(ref, ref, sem).wait()

    barrier = pltpu.get_barrier_semaphore()

    def sends_to(c0, z0, c1, z1):
        a = z1 // 4 == c0
        a = a | ((c0 == 0) & (c1 == 0) & (z1 // 4 == 1))
        a = a | (z1 == z0)
        a = a | ((c1 == c0) & (z1 // 4 == z0 // 4))
        a = a | ((c1 == z0 // 4) & (z1 // 4 == lax.rem(z0, 4) // 2))
        return a & jnp.logical_not((c0 == c1) & (z0 == z1))

    def greet(i, count):
        co, zo = i // NZ, lax.rem(i, NZ)

        @pl.when(sends_to(co, zo, c, z))
        def _():
            pl.semaphore_signal(barrier, inc=1, device_id=(2 * q + co, zo), device_id_type=MESH)

        return count + jnp.where(sends_to(c, z, co, zo), 1, 0)

    count = lax.fori_loop(0, 2 * NZ, greet, jnp.int32(0))
    right, left = place(y, x + 1, c), place(y, x - 1, c)
    up, down = place(y + 1, x, c), place(y - 1, x, c)
    for other in (right, left, up, down):
        pl.semaphore_signal(barrier, inc=1, device_id=(other, z), device_id_type=MESH)
    prev_q = lax.rem(q + 31, 32)

    @pl.when((c == 0) & (z < 4))
    def _():
        def halo_greet(r, carry):
            pl.semaphore_signal(barrier, inc=1, device_id=(2 * prev_q + 1, r), device_id_type=MESH)
            return carry

        lax.fori_loop(0, NZ, halo_greet, 0)

    pl.semaphore_wait(barrier, count + 4 + 4 * c)

    sib = 2 * q + 1 - c
    d = lax.rem(y + 4 - zc, 4)
    source = d == 0

    near, far = 4 * c, 4 * (1 - c)
    send(wc_in.at[pl.ds(far, 5)], sibc, sibw_sem.at[0], sib, z, source)
    send(wq_in.at[pl.ds(2 * (1 - c), 2)], sibq, sibw_sem.at[1], sib, z)

    q_halo = lax.rem(q + c, 32)
    for k in range(4):
        send_or_keep(lat_in.at[pl.ds(0, 2)], lat.at[pl.ds(2, 2), z], lat_sem.at[1], 2 * q, 4 * c + k)
        send_or_keep(lat_in.at[pl.ds(2, 2)], lat.at[pl.ds(2, 2), z], lat_sem.at[1], 2 * q + 1, 4 * c + k)
        send_or_keep(lat_in.at[pl.ds(2, 2)], lat.at[pl.ds(0, 2), z], lat_sem.at[0], 2 * q_halo, 4 * (1 - c) + k)

    def rows_of(slot, n=1):
        return pl.ds(pl.multiple_of(16 * slot, 16), 16 * n)

    @pl.when(source)
    def _():
        arrived(sibc, sibw_sem.at[0])
        own = 2 * x + y // 4

        def merge(i, carry):
            wall[near + i, rows_of(own), :] = wc_in[near + i] + sibc[i]
            return carry

        lax.fori_loop(0, 5, merge, 0)

    arrived(sibq, sibw_sem.at[1])
    kinds = pl.ds(2 * c, 2)
    for k in range(2):
        wq[2 * c + k, rows_of(q), :] = wq_in[2 * c + k] + sibq[k]

    slot_right = 2 * x + lax.rem(y + 8 - d, 8) // 4
    slot_left = 2 * x + lax.rem(y + 8 + 4 - d, 8) // 4
    slot_left = jnp.where(source, 2 * x + y // 4, slot_left)
    slot_far = 2 * x + 1 - y // 4
    slot_in_p = jnp.where(source, slot_far, slot_right)
    slot_in_m = slot_left

    def wpart(i, slot, n=1):
        return wall.at[near + i, rows_of(slot, n), :]

    def y_stage(i):
        @pl.when(jnp.logical_not(source))
        def _():
            arrived(wpart(i, slot_in_p), yp.at[i])

        send(wpart(i, slot_right), wpart(i, slot_right), yp.at[i], up, z)

        @pl.when(jnp.logical_not(source))
        def _():
            arrived(wpart(i, slot_in_m), ym.at[i])

        send(wpart(i, slot_left), wpart(i, slot_left), ym.at[i], down, z, d != 1)

    xl, xr, xo = lax.rem(x + 3, 4), lax.rem(x + 1, 4), lax.rem(x + 2, 4)

    def x1_stage(i):
        @pl.when(source)
        def _():
            arrived(wpart(i, slot_in_p), yp.at[i])

        send(wpart(i, 2 * x, 2), wpart(i, 2 * x, 2), xp.at[i], right, z)
        send(wpart(i, 2 * x, 2), wpart(i, 2 * x, 2), xm.at[i], left, z)

    def x2_stage(i):
        arrived(wpart(i, 2 * xl, 2), xp.at[i])
        send(wpart(i, 2 * xl), wpart(i, 2 * xl), xpp.at[i], right, z)
        arrived(wpart(i, 2 * xr, 2), xm.at[i])
        send(wpart(i, 2 * xr + 1), wpart(i, 2 * xr + 1), xmm.at[i], left, z)

    def x3_stage(i):
        arrived(wpart(i, 2 * xo), xpp.at[i])
        arrived(wpart(i, 2 * xo + 1), xmm.at[i])
        n = jnp.where(c == 0, i, i - 1)
        whole = wall.at[near + i]
        when = None if 0 < i < 4 else (c == 0 if i == 0 else c == 1)
        n = jnp.clip(n, 0, 3)
        send(whole, whole, ssib.at[n], sib, z, when)

    def qpart(k, nk, slot, n):
        return wq.at[pl.ds(2 * c + k, nk), rows_of(slot, n), :]

    row = 4 * y

    def q_stage(s):
        if s == 0:
            own = qpart(0, 2, q, 1)
            send(own, own, qx.at[0], right, z)
            send(own, own, qx.at[1], left, z)
        elif s == 1:
            arrived(qpart(0, 2, row + xl, 1), qx.at[0])
            part = qpart(0, 1, row + xl, 1)
            send(part, part, qx.at[2], right, z)
            arrived(qpart(0, 2, row + xr, 1), qx.at[1])
            part = qpart(1, 1, row + xr, 1)
            send(part, part, qx.at[3], left, z)
        elif s == 2:
            arrived(qpart(0, 1, row + xo, 1), qx.at[2])
            arrived(qpart(1, 1, row + xo, 1), qx.at[3])
            block = qpart(0, 2, row, 4)
            send(block, block, qy.at[0], up, z)
            send(block, block, qy.at[1], down, z)
        elif s < 6:
            step = s - 2
            from_p = 4 * lax.rem(y + 8 - step, 8)
            from_m = 4 * lax.rem(y + step, 8)
            arrived(qpart(0, 2, from_p, 4), qy.at[2 * step - 2])
            part = qpart(0, 2, from_p, 4) if step < 3 else qpart(0, 1, from_p, 4)
            send(part, part, qy.at[2 * step], up, z)
            arrived(qpart(0, 2, from_m, 4), qy.at[2 * step - 1])
            part = qpart(0, 2, from_m, 4) if step < 3 else qpart(1, 1, from_m, 4)
            send(part, part, qy.at[2 * step + 1], down, z)
        else:
            far_row = 4 * lax.rem(y + 4, 8)
            arrived(qpart(0, 1, far_row, 4), qy.at[6])
            arrived(qpart(1, 1, far_row, 4), qy.at[7])
            both = wq.at[kinds]
            send(both, both, qsib, sib, z)

    def constants():
        gmat[...] = one_hot(twelfth(iota((C, C), 0)) == twelfth(iota((C, C), 1)))
        zero = jnp.zeros((32, 3 * C), BF)
        for s in range(4):
            act[s, 0:32, :] = zero
            act[s, 288:320, :] = zero

    y_stage(0)
    q_stage(0)
    constants()
    y_stage(1)
    x1_stage(0)
    y_stage(2)
    q_stage(1)
    x1_stage(1)
    x2_stage(0)
    y_stage(3)
    q_stage(2)
    x1_stage(2)
    x2_stage(1)
    x3_stage(0)
    y_stage(4)
    q_stage(3)
    x1_stage(3)
    x2_stage(2)
    x3_stage(1)
    q_stage(4)
    x1_stage(4)
    x2_stage(3)
    x3_stage(2)
    q_stage(5)

    mine, halo = lat.at[pl.ds(2, 2)], lat.at[pl.ds(0, 2)]
    arrived(mine, lat_sem.at[1])
    send(mine, halo, lat_sem.at[0], sib, z, c == 0)

    x2_stage(4)
    x3_stage(3)

    def frame_sum(s, mean):
        def step(i, total):
            v = lat[s, i].astype(F32)
            if mean is not None:
                v = v - mean
                v = v * v
            return total + v

        return jnp.sum(lax.fori_loop(0, 8, step, jnp.zeros((32, C), F32)), axis=0, keepdims=True)

    col = iota((32, C), 0)

    def activate(pair):
        frames = (2 * pair, 2 * pair + 1)
        means = group_means([frame_sum(s, None) for s in frames], gmat[...])
        variances = group_means([frame_sum(s, m) for s, m in zip(frames, means)], gmat[...])
        for s, m, var in zip(frames, means, variances):
            scale = lax.rsqrt(var + 1e-06)
            gain = gain1[...]
            empty = (c == 0) & (z < 4) & (q == 0) & (s < 2)

            def step(i, carry):
                v = (lat[s, i].astype(F32) - m) * scale * gain
                v = v / (1.0 + jnp.exp(-v))
                v = jnp.where(empty, 0.0, v)
                at = pl.ds(pl.multiple_of(32 * i + 32, 32), 32)
                act[s, at, 0:C] = jnp.where(col == 0, 0.0, pltpu.roll(v, 1, 0)).astype(BF)
                act[s, at, C : 2 * C] = v.astype(BF)
                act[s, at, 2 * C : 3 * C] = jnp.where(col == 31, 0.0, pltpu.roll(v, 31, 0)).astype(BF)
                return carry

            lax.fori_loop(0, 8, step, 0)

    activate(1)
    x3_stage(4)
    arrived(halo, lat_sem.at[0])
    activate(0)

    acc[...] = jnp.zeros_like(acc)

    def taps(ta):
        t, a = ta // 3, lax.rem(ta, 3)
        for j in range(2):
            rows = pl.ds(pl.multiple_of(32 * a, 32), 256)
            acc[j] += dot_nt(act[j + t, rows, :], wall[ta])

    def own_taps(i, carry):
        taps(near + i)
        return carry

    lax.fori_loop(0, 5, own_taps, 0)

    def sib_taps(n, carry):
        ta = jnp.where(c == 0, 5 + n, n)
        arrived(wall.at[ta], ssib.at[n])
        taps(ta)
        return carry

    lax.fori_loop(0, 4, sib_taps, 0)

    lane = iota((C, 128), 1)
    slot = lane >> 4
    chan = 12 * ((zc + 4 * (slot & 1)) * 4 + (slot >> 1)) + (lane & 15)
    pick = one_hot((iota((C, 128), 0) == chan) & ((lane & 15) < 12))
    for j in range(2):
        frame = lat[2 + j].reshape(256, C)
        thr_s[j] = (dot_nn(frame, pick) + acc[j]).astype(BF)

    for k in range(4):
        j = k % 2
        dst = thr.at[:, pl.ds(pl.multiple_of(128 * zc, 128), 128)]
        send_or_keep(thr_s.at[j], dst, exsem.at[zc], tm, 4 * g + k)
    q_stage(6)
    for k in range(4):
        arrived(thr.at[:, pl.ds(128 * k, 128)], exsem.at[k])

    part = iota((512, C), 0)
    slot = (part & 127) >> 4
    chan = 12 * (((part >> 7) + 4 * (slot & 1)) * 4 + (slot >> 1)) + (part & 15)
    pick_all = one_hot((iota((512, C), 1) == chan) & ((part & 15) < 12))
    through = dot_nn(thr[...], pick_all)
    thrn[...] = through

    mean = group_means([jnp.sum(through, axis=0, keepdims=True)], gmat[...])[0]
    dev = through - mean
    var = group_means([jnp.sum(dev * dev, axis=0, keepdims=True)], gmat[...])[0]
    normed = (dev * lax.rsqrt(var + 1e-06) * gain2[...]).astype(BF)
    thr[:, 0:C] = normed

    arrived(wq.at[pl.ds(2 * (1 - c), 2)], qsib)
    packed = iota((C, 512), 1)
    unpack = one_hot((iota((C, 512), 0) == 12 * (packed >> 4) + (packed & 15)) & ((packed & 15) < 12))
    w_value = dot_nn(unpack, wq[2]).astype(BF)
    w_out = dot_nn(unpack, wq[3]).astype(BF)
    mine_rows = pl.ds(pl.multiple_of(128 * half, 128), 128)
    queries = dot_nt(thr[mine_rows, 0:C], wq[0]).astype(BF)
    keys = dot_nt(normed, wq[1]).astype(BF)
    values = dot_nt(normed, w_value).astype(BF)
    scores = dot_nt(queries, keys) * (C ** -0.5)
    expon = jnp.exp(scores - jnp.max(scores, axis=1, keepdims=True))
    totals = jnp.sum(expon, axis=1, keepdims=True)
    attended = (dot_nn(expon.astype(BF), values) / totals).astype(BF)
    result = thrn[mine_rows, :] + dot_nt(attended, w_out)
    obuf[...] = result.astype(BF).reshape(4, 32, C)

    fr = 2 * c + fsel
    for k in range(4):
        send_or_keep(obuf.at[k], out_ref.at[fr], outsem.at[fr], 2 * q + g, 4 * half + k)
    for k in range(4):
        arrived(out_ref.at[k], outsem.at[k])

    for when, desc in pending:
        if when is None:
            desc.wait_send()
        else:
            pl.when(when)(desc.wait_send)


def body(latents, gain_one, conv_weight, gain_two, qkv_weight, out_weight):
    c = lax.rem(lax.axis_index("tm"), 2)
    taps = conv_weight.reshape(9, 3, C, 6).transpose(0, 3, 1, 2).reshape(9, 6, 3 * C)
    proj = jnp.concatenate([qkv_weight.transpose(0, 2, 1), out_weight.T[None]], 0)

    def placed(w):
        low = jnp.pad(w, ((0, 0), (0, 10), (0, 0)))
        high = jnp.pad(w, ((0, 0), (6, 4), (0, 0)))
        return jnp.where(c == 0, low, high)

    vmem = pl.BlockSpec(memory_space=pltpu.VMEM)
    dma = pltpu.SemaphoreType.DMA
    out = pl.pallas_call(
        kernel,
        out_shape=jax.ShapeDtypeStruct((4, 32, C), BF),
        in_specs=[pl.BlockSpec(memory_space=pl.ANY)] + [vmem] * 4,
        out_specs=vmem,
        scratch_shapes=[
            pltpu.VMEM((4, 8, 32, C), BF),
            pltpu.VMEM((5, 16, 3 * C), BF),
            pltpu.VMEM((2, 16, C), BF),
            pltpu.VMEM((9, 128, 3 * C), BF),
            pltpu.VMEM((4, 512, C), BF),
            pltpu.VMEM((4, 320, 3 * C), BF),
            pltpu.VMEM((2, 256, 128), F32),
            pltpu.VMEM((2, 256, 128), BF),
            pltpu.VMEM((256, 512), BF),
            pltpu.VMEM((256, C), F32),
            pltpu.VMEM((4, 32, C), BF),
            pltpu.VMEM((C, C), BF),
            dma((NSEND,)), dma((2,)), dma((2,)), dma((5,)), dma((5,)), dma((5,)), dma((5,)), dma((5,)), dma((5,)),
            dma((4,)), dma((4,)), dma((8,)), dma, dma((4,)), dma((4,)),
        ],
        compiler_params=pltpu.CompilerParams(
            collective_id=0, has_side_effects=True, vmem_limit_bytes=40 * 1024 * 1024
        ),
        cost_estimate=pl.CostEstimate(flops=2 * 10**9, bytes_accessed=10**7, transcendentals=10**6),
    )(latents[:, 0], placed(taps), placed(proj), gain_one[None], gain_two[None])
    return out[:, None]


def solution(mesh):
    in_specs = (
        P("tm", "rows", None, None),
        P(),
        P(None, None, "tm"),
        P(),
        P(None, None, "tm"),
        P(None, "tm"),
    )
    out_specs = P("tm", "rows", None, None)
    return jax.shard_map(body, mesh=mesh, in_specs=in_specs, out_specs=out_specs, check_vma=False)
```

time: 367 us -> 121 us (0.33)
  the two profiles are of different devices: /device:TPU:2 before, /device:TPU:1 now
where the time goes in v1:
time: 121 us; the launch traced here: 120 us
  Pallas kernels  116 us (96%)
  local copies, waits for them, and re-layouts  3.7 us (3%)
    pallas_call x1, Pallas kernels, body(): pl.pallas_call(kernel, out_shape=jax.ShapeDtypeStruct((4, 32, C), BF), in...  116 us
    unnamed x11, local copies, waits for them, and re-layouts  2.55 us

profile of v1, /device:TPU:1, one launch (start us, length us, event | category | flops | bytes accessed | tf_op | source)
XLA Modules:
  0.0 120.3 jit_solution(1485299889357512279)
XLA Ops:
  0.0 1.0 reshape.6
  1.0 0.1 copy.10
  1.0 0.1 reshape.7
  1.2 0.0 copy-start.1
  1.2 0.0 copy-start.2
  1.2 0.1 pad_select_fusion.wc_in
  1.3 0.0 copy-start
  1.3 0.6 copy-done.1
  1.9 0.0 copy-done.2
  1.9 0.0 copy-start.3
  1.9 0.6 copy-done.3
  2.6 0.0 copy-start.4
  2.6 0.7 copy-done.4
  3.3 0.0 copy-done
  3.3 116.4 %shard_map.64 = bf16[4,32,384]{2,1,0:T(8,128)(2,1)S(1)} custom-call(bf16[4,32,384]{2,1,0:T(8,128)(2,1)S(1)} %bitcast.14, bf16[9,16,1152]{2,1,0:T(8,128)(2,1)S(1)} %pad_select_fusion.wc_in, bf16[4,16,384]{2,1,0:T(8,128)(2,1)S(1)} %pad_select_fusion.1.wq_in, f32[1,384]{1,0:T(1,128)S(1)} %broadcast_in_dim.13.gain1, f32[1,384]{1,0:T(1,128)S(1)} %broadcast_in_dim.14.gain2), custom_call_target="tpu_custom_call" | custom-call | flops 2000000000 | bytes 10000000 | tf_op jit(solution)/shard_map/pallas_call | solution.py:419
  119.7 0.6 copy.12
  (4 shorter events, 0.0 us)
Async XLA Ops:
  1.2 0.7 copy-start.1
  1.2 0.7 copy-start.2
  1.3 2.0 %copy-start = (bf16[4,1,32,384]{3,2,1,0:T(8,128)(2,1)S(1)}, bf16[4,1,32,384]{3,2,1,0:T(8,128)(2,1)}, u32[]{:S(2)}) copy-start(bf16[4,1,32,384]{3,2,1,0:T(8,128)(2,1)} %param.6) | copy-start | bytes 294916
  1.9 0.7 copy-start.3
  2.6 0.7 copy-start.4

commit v2 on v1

--- a/solution.py
+++ b/solution.py
@@ -169,18 +169,51 @@
     def wpart(i, slot, n=1):
         return wall.at[near + i, rows_of(slot, n), :]
 
-    def y_stage(i):
-        @pl.when(jnp.logical_not(source))
-        def _():
-            arrived(wpart(i, slot_in_p), yp.at[i])
-
-        send(wpart(i, slot_right), wpart(i, slot_right), yp.at[i], up, z)
-
-        @pl.when(jnp.logical_not(source))
-        def _():
+    def post(src, rsem, to_tm, index):
+        return pltpu.make_async_remote_copy(
+            src_ref=src, dst_ref=src, send_sem=sends.at[index], recv_sem=rsem,
+            device_id=(to_tm, z), device_id_type=MESH,
+        )
+
+    first_y = len(pending)
+    ups = [post(wpart(i, slot_right), yp.at[i], up, first_y + i) for i in range(5)]
+    downs = [post(wpart(i, slot_left), ym.at[i], down, first_y + 5 + i) for i in range(5)]
+    pending.extend((None, d_up) for d_up in ups)
+    pending.extend((d != 1, d_down) for d_down in downs)
+
+    def go_up(i):
+        arrived(wpart(i, slot_in_p), yp.at[i])
+        ups[i].start()
+
+    def go_down(i):
+        arrived(wpart(i, slot_in_m), ym.at[i])
+        downs[i].start()
+
+    @pl.when(source)
+    def _():
+        for i in range(5):
+            ups[i].start()
+            downs[i].start()
+
+    @pl.when(d == 1)
+    def _():
+        for i in range(5):
+            go_up(i)
+        for i in range(5):
             arrived(wpart(i, slot_in_m), ym.at[i])
 
-        send(wpart(i, slot_left), wpart(i, slot_left), ym.at[i], down, z, d != 1)
+    @pl.when(d == 2)
+    def _():
+        for i in range(5):
+            go_up(i)
+            go_down(i)
+
+    @pl.when(d == 3)
+    def _():
+        for i in range(5):
+            go_down(i)
+        for i in range(5):
+            go_up(i)
 
     xl, xr, xo = lax.rem(x + 3, 4), lax.rem(x + 1, 4), lax.rem(x + 2, 4)
 
@@ -254,37 +287,23 @@
             act[s, 0:32, :] = zero
             act[s, 288:320, :] = zero
 
-    y_stage(0)
     q_stage(0)
     constants()
-    y_stage(1)
-    x1_stage(0)
-    y_stage(2)
+    for i in range(5):
+        x1_stage(i)
     q_stage(1)
-    x1_stage(1)
-    x2_stage(0)
-    y_stage(3)
+    for i in range(5):
+        x2_stage(i)
     q_stage(2)
-    x1_stage(2)
-    x2_stage(1)
-    x3_stage(0)
-    y_stage(4)
-    q_stage(3)
-    x1_stage(3)
-    x2_stage(2)
-    x3_stage(1)
-    q_stage(4)
-    x1_stage(4)
-    x2_stage(3)
-    x3_stage(2)
-    q_stage(5)
 
     mine, halo = lat.at[pl.ds(2, 2)], lat.at[pl.ds(0, 2)]
     arrived(mine, lat_sem.at[1])
     send(mine, halo, lat_sem.at[0], sib, z, c == 0)
 
-    x2_stage(4)
-    x3_stage(3)
+    q_stage(3)
+    for i in range(4):
+        x3_stage(i)
+    q_stage(4)
 
     def frame_sum(s, mean):
         def step(i, total):
@@ -321,6 +340,7 @@
 
     activate(1)
     x3_stage(4)
+    q_stage(5)
     arrived(halo, lat_sem.at[0])
     activate(0)
 

time: 121 us -> 75.9 us (0.63)
  Pallas kernels: 116 us -> 71.8 us
    pallas_call x1, Pallas kernels: 116 us -> 71.8 us  [body(): pl.pallas_call(kernel, out_shape=jax.ShapeDtypeStruct((4, 32, C), BF), in...]
where the time goes in v2:
time: 75.9 us; the launch traced here: 75.7 us
  Pallas kernels  71.8 us (95%)
  local copies, waits for them, and re-layouts  3.7 us (5%)
    pallas_call x1, Pallas kernels, body(): pl.pallas_call(kernel, out_shape=jax.ShapeDtypeStruct((4, 32, C), BF), in...  71.8 us
    unnamed x11, local copies, waits for them, and re-layouts  2.55 us

profile of v2, /device:TPU:1, one launch (start us, length us, event | category | flops | bytes accessed | tf_op | source)
XLA Modules:
  0.0 75.7 jit_solution(8790714515461422742)
XLA Ops:
  0.0 1.0 %reshape.6 = bf16[9,3,384,6]{2,1,0,3:T(4,128)(2,1)S(1)} reshape(bf16[27,384,6]{1,0,2:T(8,128)(2,1)} %param.8) | data formatting | bytes 248832 | tf_op jit(solution)/shard_map/reshape | solution.py:429
  1.0 0.1 copy.10
  1.0 0.1 reshape.7
  1.2 0.0 copy-start.1
  1.2 0.0 copy-start.2
  1.2 0.1 pad_select_fusion.wc_in
  1.3 0.0 copy-start
  1.3 0.6 copy-done.1
  1.9 0.0 copy-done.2
  1.9 0.0 copy-start.3
  1.9 0.6 copy-done.3
  2.6 0.0 copy-start.4
  2.6 0.7 copy-done.4
  3.3 0.0 copy-done
  3.3 71.8 %shard_map.64 = bf16[4,32,384]{2,1,0:T(8,128)(2,1)S(1)} custom-call(bf16[4,32,384]{2,1,0:T(8,128)(2,1)S(1)} %bitcast.14, bf16[9,16,1152]{2,1,0:T(8,128)(2,1)S(1)} %pad_select_fusion.wc_in, bf16[4,16,384]{2,1,0:T(8,128)(2,1)S(1)} %pad_select_fusion.1.wq_in, f32[1,384]{1,0:T(1,128)S(1)} %broadcast_in_dim.13.gain1, f32[1,384]{1,0:T(1,128)S(1)} %broadcast_in_dim.14.gain2), custom_call_target="tpu_custom_call" | custom-call | flops 2000000000 | bytes 10000000 | tf_op jit(solution)/shard_map/pallas_call | solution.py:439
  75.1 0.6 copy.12
  (4 shorter events, 0.0 us)
Async XLA Ops:
  1.2 0.7 copy-start.1
  1.2 0.7 copy-start.2
  1.3 2.0 %copy-start = (bf16[4,1,32,384]{3,2,1,0:T(8,128)(2,1)S(1)}, bf16[4,1,32,384]{3,2,1,0:T(8,128)(2,1)}, u32[]{:S(2)}) copy-start(bf16[4,1,32,384]{3,2,1,0:T(8,128)(2,1)} %param.6) | copy-start | bytes 294916
  1.9 0.7 copy-start.3
  2.6 0.7 copy-start.4

commit v3 on v1

--- a/solution.py
+++ b/solution.py
@@ -51,9 +51,9 @@
 
 
 def kernel(
-    lat_in, wc_in, wq_in, gain1, gain2, out_ref,
-    lat, sibc, sibq, wall, wq, act, acc, thr_s, thr, thrn, obuf, gmat,
-    sends, lat_sem, sibw_sem, yp, ym, xp, xm, xpp, xmm, ssib, qx, qy, qsib, exsem, outsem,
+    lat_in, wc_in, wq_in, gain1_in, gain2_in, out_ref,
+    lat, sibc, sibq, own, wall, wq, act, acc, thr_s, thr, thrn, obuf, gmat, pick, pick_all, unpack, gain1, gain2,
+    sends, lat_sem, sibw_sem, yp, ym, xp, xm, xpp, xmm, ssib, qx, qy, qsib, exsem, outsem, gain_sem,
 ):
     tm = lax.axis_index("tm")
     z = lax.axis_index("rows")
@@ -90,6 +90,9 @@
     def arrived(ref, sem):
         pltpu.make_async_copy(ref, ref, sem).wait()
 
+    for k, (src, dst) in enumerate(((gain1_in, gain1), (gain2_in, gain2))):
+        pltpu.make_async_copy(src, dst, gain_sem.at[k]).start()
+
     barrier = pltpu.get_barrier_semaphore()
 
     def sends_to(c0, z0, c1, z1):
@@ -111,9 +114,19 @@
 
     count = lax.fori_loop(0, 2 * NZ, greet, jnp.int32(0))
     right, left = place(y, x + 1, c), place(y, x - 1, c)
-    up, down = place(y + 1, x, c), place(y - 1, x, c)
-    for other in (right, left, up, down):
+    near_y = [place(y + step, x, c) for step in (1, -1, 2, -2)]
+    for other in [right, left] + near_y:
         pl.semaphore_signal(barrier, inc=1, device_id=(other, z), device_id_type=MESH)
+
+    @pl.when(zc == 0)
+    def _():
+        pl.semaphore_signal(barrier, inc=1, device_id=(place(y + 4, x, c), z), device_id_type=MESH)
+
+    @pl.when(zc == 3)
+    def _():
+        for step in (3, -3):
+            pl.semaphore_signal(barrier, inc=1, device_id=(place(y + step, x, c), z), device_id_type=MESH)
+
     prev_q = lax.rem(q + 31, 32)
 
     @pl.when((c == 0) & (z < 4))
@@ -124,14 +137,13 @@
 
         lax.fori_loop(0, NZ, halo_greet, 0)
 
-    pl.semaphore_wait(barrier, count + 4 + 4 * c)
+    pl.semaphore_wait(barrier, count + 6 + 4 * c + jnp.where(zc == 0, 1, 0) + jnp.where(zc == 3, 2, 0))
 
     sib = 2 * q + 1 - c
-    d = lax.rem(y + 4 - zc, 4)
-    source = d == 0
+    far_row = jnp.where(zc == 0, 4, -zc)
 
     near, far = 4 * c, 4 * (1 - c)
-    send(wc_in.at[pl.ds(far, 5)], sibc, sibw_sem.at[0], sib, z, source)
+    send(wc_in.at[pl.ds(far, 5)], sibc, sibw_sem.at[0], sib, z)
     send(wq_in.at[pl.ds(2 * (1 - c), 2)], sibq, sibw_sem.at[1], sib, z)
 
     q_halo = lax.rem(q + c, 32)
@@ -143,54 +155,56 @@
     def rows_of(slot, n=1):
         return pl.ds(pl.multiple_of(16 * slot, 16), 16 * n)
 
-    @pl.when(source)
-    def _():
-        arrived(sibc, sibw_sem.at[0])
-        own = 2 * x + y // 4
-
-        def merge(i, carry):
-            wall[near + i, rows_of(own), :] = wc_in[near + i] + sibc[i]
-            return carry
-
-        lax.fori_loop(0, 5, merge, 0)
+    kinds = pl.ds(2 * c, 2)
+
+    def wpart(i, slot, n=1):
+        return wall.at[near + i, rows_of(slot, n), :]
+
+    def post(src, rsem, to_tm, index):
+        return pltpu.make_async_remote_copy(
+            src_ref=src, dst_ref=src, send_sem=sends.at[index], recv_sem=rsem,
+            device_id=(to_tm, z), device_id_type=MESH,
+        )
+
+    to_first, to_second = place(y - zc, x, c), place(y - far_row, x, c)
+    arrived(sibc, sibw_sem.at[0])
+    for i in range(5):
+        own[i] = wc_in[near + i] + sibc[i]
+        for h, (to, sem) in enumerate(((to_first, yp), (to_second, ym))):
+            copy = pltpu.make_async_remote_copy(
+                src_ref=own.at[i], dst_ref=wpart(i, 2 * x + h), send_sem=sends.at[len(pending)],
+                recv_sem=sem.at[i], device_id=(to, z), device_id_type=MESH,
+            )
+            when = zc != 0 if h == 0 else None
+            if h == 0:
+                pl.when(zc != 0)(copy.start)
+            else:
+                copy.start()
+            pending.append((when, copy))
 
     arrived(sibq, sibw_sem.at[1])
-    kinds = pl.ds(2 * c, 2)
     for k in range(2):
         wq[2 * c + k, rows_of(q), :] = wq_in[2 * c + k] + sibq[k]
 
-    slot_right = 2 * x + lax.rem(y + 8 - d, 8) // 4
-    slot_left = 2 * x + lax.rem(y + 8 + 4 - d, 8) // 4
-    slot_left = jnp.where(source, 2 * x + y // 4, slot_left)
-    slot_far = 2 * x + 1 - y // 4
-    slot_in_p = jnp.where(source, slot_far, slot_right)
-    slot_in_m = slot_left
-
-    def wpart(i, slot, n=1):
-        return wall.at[near + i, rows_of(slot, n), :]
-
-    def y_stage(i):
-        @pl.when(jnp.logical_not(source))
+    xl, xr, xo = lax.rem(x + 3, 4), lax.rem(x + 1, 4), lax.rem(x + 2, 4)
+
+    first_x = len(pending)
+    rights = [post(wpart(i, 2 * x, 2), xp.at[i], right, first_x + i) for i in range(5)]
+    lefts = [post(wpart(i, 2 * x, 2), xm.at[i], left, first_x + 5 + i) for i in range(5)]
+    pending.extend((None, copy) for copy in rights + lefts)
+
+    def x1_stage(i):
+        @pl.when(zc == 0)
         def _():
-            arrived(wpart(i, slot_in_p), yp.at[i])
-
-        send(wpart(i, slot_right), wpart(i, slot_right), yp.at[i], up, z)
-
-        @pl.when(jnp.logical_not(source))
+            wall[near + i, rows_of(2 * x), :] = own[i]
+
+        @pl.when(zc != 0)
         def _():
-            arrived(wpart(i, slot_in_m), ym.at[i])
-
-        send(wpart(i, slot_left), wpart(i, slot_left), ym.at[i], down, z, d != 1)
-
-    xl, xr, xo = lax.rem(x + 3, 4), lax.rem(x + 1, 4), lax.rem(x + 2, 4)
-
-    def x1_stage(i):
-        @pl.when(source)
-        def _():
-            arrived(wpart(i, slot_in_p), yp.at[i])
-
-        send(wpart(i, 2 * x, 2), wpart(i, 2 * x, 2), xp.at[i], right, z)
-        send(wpart(i, 2 * x, 2), wpart(i, 2 * x, 2), xm.at[i], left, z)
+            arrived(wpart(i, 2 * x), yp.at[i])
+
+        arrived(wpart(i, 2 * x + 1), ym.at[i])
+        rights[i].start()
+        lefts[i].start()
 
     def x2_stage(i):
         arrived(wpart(i, 2 * xl, 2), xp.at[i])
@@ -211,6 +225,9 @@
         return wq.at[pl.ds(2 * c + k, nk), rows_of(slot, n), :]
 
     row = 4 * y
+
+    def q_row(step):
+        return 4 * lax.rem(y + 8 + step, 8)
 
     def q_stage(s):
         if s == 0:
@@ -228,22 +245,17 @@
             arrived(qpart(0, 1, row + xo, 1), qx.at[2])
             arrived(qpart(1, 1, row + xo, 1), qx.at[3])
             block = qpart(0, 2, row, 4)
-            send(block, block, qy.at[0], up, z)
-            send(block, block, qy.at[1], down, z)
-        elif s < 6:
-            step = s - 2
-            from_p = 4 * lax.rem(y + 8 - step, 8)
-            from_m = 4 * lax.rem(y + step, 8)
-            arrived(qpart(0, 2, from_p, 4), qy.at[2 * step - 2])
-            part = qpart(0, 2, from_p, 4) if step < 3 else qpart(0, 1, from_p, 4)
-            send(part, part, qy.at[2 * step], up, z)
-            arrived(qpart(0, 2, from_m, 4), qy.at[2 * step - 1])
-            part = qpart(0, 2, from_m, 4) if step < 3 else qpart(1, 1, from_m, 4)
-            send(part, part, qy.at[2 * step + 1], down, z)
+            for n in range(4):
+                send(block, block, qy.at[n], near_y[n], z)
+        elif s == 3:
+            for n, step in enumerate((-1, 1, -2, 2)):
+                arrived(qpart(0, 2, q_row(step), 4), qy.at[n])
+            for n, (step, k, nk) in enumerate(((-1, 0, 2), (1, 0, 2), (-2, 0, 1), (2, 1, 1))):
+                block = qpart(k, nk, q_row(step), 4)
+                send(block, block, qy.at[4 + n], near_y[2 + n % 2], z)
         else:
-            far_row = 4 * lax.rem(y + 4, 8)
-            arrived(qpart(0, 1, far_row, 4), qy.at[6])
-            arrived(qpart(1, 1, far_row, 4), qy.at[7])
+            for n, (step, k, nk) in enumerate(((-3, 0, 2), (3, 0, 2), (4, 0, 1), (4, 1, 1))):
+                arrived(qpart(k, nk, q_row(step), 4), qy.at[4 + n])
             both = wq.at[kinds]
             send(both, both, qsib, sib, z)
 
@@ -253,38 +265,21 @@
         for s in range(4):
             act[s, 0:32, :] = zero
             act[s, 288:320, :] = zero
-
-    y_stage(0)
-    q_stage(0)
-    constants()
-    y_stage(1)
-    x1_stage(0)
-    y_stage(2)
-    q_stage(1)
-    x1_stage(1)
-    x2_stage(0)
-    y_stage(3)
-    q_stage(2)
-    x1_stage(2)
-    x2_stage(1)
-    x3_stage(0)
-    y_stage(4)
-    q_stage(3)
-    x1_stage(3)
-    x2_stage(2)
-    x3_stage(1)
-    q_stage(4)
-    x1_stage(4)
-    x2_stage(3)
-    x3_stage(2)
-    q_stage(5)
+        def channel(place_in, k):
+            slot = (place_in & 127) >> 4
+            row_of = (y + 8 + jnp.where((slot & 1) == 0, k, jnp.where(k == 0, 4, -k))) & 7
+            return 12 * (row_of * 4 + (slot >> 1)) + (place_in & 15)
+
+        lane = iota((C, 128), 1)
+        chan = channel(lane, zc)
+        pick[...] = one_hot((iota((C, 128), 0) == chan) & ((lane & 15) < 12))
+        part = iota((512, C), 0)
+        chan = channel(part, part >> 7)
+        pick_all[...] = one_hot((iota((512, C), 1) == chan) & ((part & 15) < 12))
+        packed = iota((C, 512), 1)
+        unpack[...] = one_hot((iota((C, 512), 0) == 12 * (packed >> 4) + (packed & 15)) & ((packed & 15) < 12))
 
     mine, halo = lat.at[pl.ds(2, 2)], lat.at[pl.ds(0, 2)]
-    arrived(mine, lat_sem.at[1])
-    send(mine, halo, lat_sem.at[0], sib, z, c == 0)
-
-    x2_stage(4)
-    x3_stage(3)
 
     def frame_sum(s, mean):
         def step(i, total):
@@ -304,7 +299,7 @@
         variances = group_means([frame_sum(s, m) for s, m in zip(frames, means)], gmat[...])
         for s, m, var in zip(frames, means, variances):
             scale = lax.rsqrt(var + 1e-06)
-            gain = gain1[...]
+            gain = gain1[...].reshape(1, C)
             empty = (c == 0) & (z < 4) & (q == 0) & (s < 2)
 
             def step(i, carry):
@@ -319,24 +314,46 @@
 
             lax.fori_loop(0, 8, step, 0)
 
-    activate(1)
-    x3_stage(4)
-    arrived(halo, lat_sem.at[0])
-    activate(0)
-
-    acc[...] = jnp.zeros_like(acc)
-
     def taps(ta):
         t, a = ta // 3, lax.rem(ta, 3)
         for j in range(2):
             rows = pl.ds(pl.multiple_of(32 * a, 32), 256)
             acc[j] += dot_nt(act[j + t, rows, :], wall[ta])
 
-    def own_taps(i, carry):
+    def own_taps(i):
+        x3_stage(i)
         taps(near + i)
-        return carry
-
-    lax.fori_loop(0, 5, own_taps, 0)
+
+    q_stage(0)
+    constants()
+    arrived(gain1, gain_sem.at[0])
+    arrived(gain2, gain_sem.at[1])
+    x1_stage(0)
+    x1_stage(1)
+    q_stage(1)
+    x1_stage(2)
+    x2_stage(0)
+    x1_stage(3)
+    x2_stage(1)
+    q_stage(2)
+    x1_stage(4)
+    x2_stage(2)
+    arrived(mine, lat_sem.at[1])
+    send(mine, halo, lat_sem.at[0], sib, z, c == 0)
+    for j in range(2):
+        acc[j] = dot_nn(lat[2 + j].reshape(256, C), pick[...])
+    activate(1)
+    x2_stage(3)
+    q_stage(3)
+    arrived(halo, lat_sem.at[0])
+    activate(0)
+    x2_stage(4)
+    own_taps(0)
+    own_taps(1)
+    q_stage(4)
+    own_taps(2)
+    own_taps(3)
+    own_taps(4)
 
     def sib_taps(n, carry):
         ta = jnp.where(c == 0, 5 + n, n)
@@ -345,41 +362,28 @@
         return carry
 
     lax.fori_loop(0, 4, sib_taps, 0)
-
-    lane = iota((C, 128), 1)
-    slot = lane >> 4
-    chan = 12 * ((zc + 4 * (slot & 1)) * 4 + (slot >> 1)) + (lane & 15)
-    pick = one_hot((iota((C, 128), 0) == chan) & ((lane & 15) < 12))
     for j in range(2):
-        frame = lat[2 + j].reshape(256, C)
-        thr_s[j] = (dot_nn(frame, pick) + acc[j]).astype(BF)
+        thr_s[j] = acc[j].astype(BF)
 
     for k in range(4):
         j = k % 2
         dst = thr.at[:, pl.ds(pl.multiple_of(128 * zc, 128), 128)]
         send_or_keep(thr_s.at[j], dst, exsem.at[zc], tm, 4 * g + k)
-    q_stage(6)
+    arrived(wq.at[pl.ds(2 * (1 - c), 2)], qsib)
+    w_value = dot_nn(unpack[...], wq[2]).astype(BF)
+    w_out = dot_nn(unpack[...], wq[3]).astype(BF)
     for k in range(4):
         arrived(thr.at[:, pl.ds(128 * k, 128)], exsem.at[k])
 
-    part = iota((512, C), 0)
-    slot = (part & 127) >> 4
-    chan = 12 * (((part >> 7) + 4 * (slot & 1)) * 4 + (slot >> 1)) + (part & 15)
-    pick_all = one_hot((iota((512, C), 1) == chan) & ((part & 15) < 12))
-    through = dot_nn(thr[...], pick_all)
+    through = dot_nn(thr[...], pick_all[...])
     thrn[...] = through
 
     mean = group_means([jnp.sum(through, axis=0, keepdims=True)], gmat[...])[0]
     dev = through - mean
     var = group_means([jnp.sum(dev * dev, axis=0, keepdims=True)], gmat[...])[0]
-    normed = (dev * lax.rsqrt(var + 1e-06) * gain2[...]).astype(BF)
+    normed = (dev * lax.rsqrt(var + 1e-06) * gain2[...].reshape(1, C)).astype(BF)
     thr[:, 0:C] = normed
 
-    arrived(wq.at[pl.ds(2 * (1 - c), 2)], qsib)
-    packed = iota((C, 512), 1)
-    unpack = one_hot((iota((C, 512), 0) == 12 * (packed >> 4) + (packed & 15)) & ((packed & 15) < 12))
-    w_value = dot_nn(unpack, wq[2]).astype(BF)
-    w_out = dot_nn(unpack, wq[3]).astype(BF)
     mine_rows = pl.ds(pl.multiple_of(128 * half, 128), 128)
     queries = dot_nt(thr[mine_rows, 0:C], wq[0]).astype(BF)
     keys = dot_nt(normed, wq[1]).astype(BF)
@@ -415,16 +419,18 @@
         return jnp.where(c == 0, low, high)
 
     vmem = pl.BlockSpec(memory_space=pltpu.VMEM)
+    anywhere = pl.BlockSpec(memory_space=pl.ANY)
     dma = pltpu.SemaphoreType.DMA
     out = pl.pallas_call(
         kernel,
         out_shape=jax.ShapeDtypeStruct((4, 32, C), BF),
-        in_specs=[pl.BlockSpec(memory_space=pl.ANY)] + [vmem] * 4,
+        in_specs=[anywhere, vmem, vmem, anywhere, anywhere],
         out_specs=vmem,
         scratch_shapes=[
             pltpu.VMEM((4, 8, 32, C), BF),
             pltpu.VMEM((5, 16, 3 * C), BF),
             pltpu.VMEM((2, 16, C), BF),
+            pltpu.VMEM((5, 16, 3 * C), BF),
             pltpu.VMEM((9, 128, 3 * C), BF),
             pltpu.VMEM((4, 512, C), BF),
             pltpu.VMEM((4, 320, 3 * C), BF),
@@ -434,14 +440,19 @@
             pltpu.VMEM((256, C), F32),
             pltpu.VMEM((4, 32, C), BF),
             pltpu.VMEM((C, C), BF),
+            pltpu.VMEM((C, 128), BF),
+            pltpu.VMEM((512, C), BF),
+            pltpu.VMEM((C, 512), BF),
+            pltpu.VMEM((C,), F32),
+            pltpu.VMEM((C,), F32),
             dma((NSEND,)), dma((2,)), dma((2,)), dma((5,)), dma((5,)), dma((5,)), dma((5,)), dma((5,)), dma((5,)),
-            dma((4,)), dma((4,)), dma((8,)), dma, dma((4,)), dma((4,)),
+            dma((4,)), dma((4,)), dma((8,)), dma, dma((4,)), dma((4,)), dma((2,)),
         ],
         compiler_params=pltpu.CompilerParams(
             collective_id=0, has_side_effects=True, vmem_limit_bytes=40 * 1024 * 1024
         ),
         cost_estimate=pl.CostEstimate(flops=2 * 10**9, bytes_accessed=10**7, transcendentals=10**6),
-    )(latents[:, 0], placed(taps), placed(proj), gain_one[None], gain_two[None])
+    )(latents[:, 0], placed(taps), placed(proj), gain_one, gain_two)
     return out[:, None]
 
 

time: 121 us -> 67.3 us (0.56)
  Pallas kernels: 116 us -> 63.8 us
    pallas_call x1, Pallas kernels: 116 us -> 63.8 us  [body(): pl.pallas_call(kernel, out_shape=jax.ShapeDtypeStruct((4, 32, C), BF), in...]
where the time goes in v3:
time: 67.3 us; the launch traced here: 67.1 us
  Pallas kernels  63.8 us (95%)
  local copies, waits for them, and re-layouts  3.04 us (5%)
    pallas_call x1, Pallas kernels, body(): pl.pallas_call(kernel, out_shape=jax.ShapeDtypeStruct((4, 32, C), BF), in...  63.8 us
    unnamed x11, local copies, waits for them, and re-layouts  1.89 us

profile of v3, /device:TPU:1, one launch (start us, length us, event | category | flops | bytes accessed | tf_op | source)
XLA Modules:
  0.0 67.1 jit_solution(5168966320668242920)
XLA Ops:
  0.0 1.0 %reshape.6 = bf16[9,3,384,6]{2,1,0,3:T(4,128)(2,1)S(1)} reshape(bf16[27,384,6]{1,0,2:T(8,128)(2,1)} %param.8) | data formatting | bytes 248832 | tf_op jit(solution)/shard_map/reshape | solution.py:413
  1.0 0.1 copy.10
  1.0 0.1 reshape.7
  1.2 0.0 copy-start.3
  1.2 0.0 copy-start.4
  1.2 0.1 pad_select_fusion.wc_in
  1.3 0.0 copy-start
  1.3 0.6 copy-done.3
  1.9 0.0 copy-done.4
  1.9 0.0 copy-start.1
  1.9 0.0 copy-start.2
  2.0 0.2 copy-done
  2.2 0.4 copy-done.1
  2.6 0.0 copy-done.2
  2.6 63.8 %shard_map.64 = bf16[4,32,384]{2,1,0:T(8,128)(2,1)S(1)} custom-call(bf16[4,32,384]{2,1,0:T(8,128)(2,1)S(1)} %bitcast.14, bf16[9,16,1152]{2,1,0:T(8,128)(2,1)S(1)} %pad_select_fusion.wc_in, bf16[4,16,384]{2,1,0:T(8,128)(2,1)S(1)} %pad_select_fusion.1.wq_in, f32[384]{0:T(512)S(1)} %copy-done.1, f32[384]{0:T(512)S(1)} %copy-done.2), custom_call_target="tpu_custom_call" | custom-call | flops 2000000000 | bytes 10000000 | tf_op jit(solution)/shard_map/pallas_call | solution.py:424
  66.5 0.6 copy.12
  (2 shorter events, 0.0 us)
Async XLA Ops:
  1.2 0.7 %copy-start.3 = (bf16[3,384,6]{1,2,0:T(8,128)(2,1)S(1)}, bf16[3,384,6]{1,2,0:T(8,128)(2,1)}, u32[]{:S(2)}) copy-start(bf16[3,384,6]{1,2,0:T(8,128)(2,1)} %param.10) | copy-start | bytes 41476
  1.2 0.7 %copy-start.4 = (bf16[384,6]{0,1:T(8,128)(2,1)S(1)}, bf16[384,6]{0,1:T(8,128)(2,1)}, u32[]{:S(2)}) copy-start(bf16[384,6]{0,1:T(8,128)(2,1)} %param.11) | copy-start | bytes 13828
  1.3 0.9 %copy-start = (bf16[4,1,32,384]{3,2,1,0:T(8,128)(2,1)S(1)}, bf16[4,1,32,384]{3,2,1,0:T(8,128)(2,1)}, u32[]{:S(2)}) copy-start(bf16[4,1,32,384]{3,2,1,0:T(8,128)(2,1)} %param.6) | copy-start | bytes 294916
  1.9 0.7 %copy-start.1 = (f32[384]{0:T(512)S(1)}, f32[384]{0:T(512)}, u32[]{:S(2)}) copy-start(f32[384]{0:T(512)} %gain1_in.1) | copy-start | bytes 4612
  1.9 0.7 %copy-start.2 = (f32[384]{0:T(512)S(1)}, f32[384]{0:T(512)}, u32[]{:S(2)}) copy-start(f32[384]{0:T(512)} %gain2_in.1) | copy-start | bytes 4612

commit v4 on v3

--- a/solution.py
+++ b/solution.py
@@ -52,8 +52,8 @@
 
 def kernel(
     lat_in, wc_in, wq_in, gain1_in, gain2_in, out_ref,
-    lat, sibc, sibq, own, wall, wq, act, acc, thr_s, thr, thrn, obuf, gmat, pick, pick_all, unpack, gain1, gain2,
-    sends, lat_sem, sibw_sem, yp, ym, xp, xm, xpp, xmm, ssib, qx, qy, qsib, exsem, outsem, gain_sem,
+    lat, wc, sibc, sibq, own, mid, wall, wq, act, acc, thr_s, thr, thrn, obuf, gmat, pick, pick_all, unpack, widen, gain1, gain2,
+    sends, lat_sem, sibw_sem, yp, ym, xp, xm, xpp, xmm, ssib, qx, qy, qsib, exsem, outsem, gain_sem, mid_sem,
 ):
     tm = lax.axis_index("tm")
     z = lax.axis_index("rows")
@@ -118,10 +118,6 @@
     for other in [right, left] + near_y:
         pl.semaphore_signal(barrier, inc=1, device_id=(other, z), device_id_type=MESH)
 
-    @pl.when(zc == 0)
-    def _():
-        pl.semaphore_signal(barrier, inc=1, device_id=(place(y + 4, x, c), z), device_id_type=MESH)
-
     @pl.when(zc == 3)
     def _():
         for step in (3, -3):
@@ -137,13 +133,24 @@
 
         lax.fori_loop(0, NZ, halo_greet, 0)
 
-    pl.semaphore_wait(barrier, count + 6 + 4 * c + jnp.where(zc == 0, 1, 0) + jnp.where(zc == 3, 2, 0))
+    raw = wc_in[...].reshape(192, C)
+    r16, unit = iota((112, 192), 0) & 15, iota((112, 192), 0) >> 4
+    third = twelfth(4 * unit)
+    tail = r16 >= 12
+    chan_of = jnp.where(tail, 4 * (unit - 3 * third) + r16 - 12, r16)
+    tap_row = jnp.where(tail, 7 + third, unit)
+    shard_row, tap = iota((112, 192), 1) >> 5, iota((112, 192), 1) & 31
+    for b in range(3):
+        wanted = (chan_of == 6 * c + shard_row) & (tap == 3 * tap_row + b) & (tap_row < 9)
+        wc[:, :, b * C : (b + 1) * C] = dot_nn(one_hot(wanted), raw).astype(BF).reshape(7, 16, C)
+
+    pl.semaphore_wait(barrier, count + 6 + 4 * c + jnp.where(zc == 3, 2, 0))
 
     sib = 2 * q + 1 - c
     far_row = jnp.where(zc == 0, 4, -zc)
 
-    near, far = 4 * c, 4 * (1 - c)
-    send(wc_in.at[pl.ds(far, 5)], sibc, sibw_sem.at[0], sib, z)
+    near, far = 3 * c, 3 * (1 - c)
+    send(wc.at[pl.ds(far, 4)], sibc, sibw_sem.at[0], sib, z)
     send(wq_in.at[pl.ds(2 * (1 - c), 2)], sibq, sibw_sem.at[1], sib, z)
 
     q_halo = lax.rem(q + c, 32)
@@ -168,19 +175,36 @@
 
     to_first, to_second = place(y - zc, x, c), place(y - far_row, x, c)
     arrived(sibc, sibw_sem.at[0])
-    for i in range(5):
-        own[i] = wc_in[near + i] + sibc[i]
+    for i in range(4):
+        own[i] = wc[near + i] + sibc[i]
         for h, (to, sem) in enumerate(((to_first, yp), (to_second, ym))):
             copy = pltpu.make_async_remote_copy(
                 src_ref=own.at[i], dst_ref=wpart(i, 2 * x + h), send_sem=sends.at[len(pending)],
                 recv_sem=sem.at[i], device_id=(to, z), device_id_type=MESH,
             )
-            when = zc != 0 if h == 0 else None
-            if h == 0:
-                pl.when(zc != 0)(copy.start)
-            else:
-                copy.start()
-            pending.append((when, copy))
+            pl.when(zc != 0)(copy.start)
+            pending.append((zc != 0, copy))
+
+    hops = []
+    for i in range(4):
+        for src, dst, sem in ((own.at[i], mid.at[i], mid_sem), (mid.at[i], wpart(i, 2 * x + 1), ym)):
+            copy = pltpu.make_async_remote_copy(
+                src_ref=src, dst_ref=dst, send_sem=sends.at[len(pending)], recv_sem=sem.at[i],
+                device_id=(near_y[2 + i % 2], z), device_id_type=MESH,
+            )
+            pending.append((zc == 0, copy))
+            hops.append(copy)
+
+    @pl.when(zc == 0)
+    def _():
+        for i in range(4):
+            hops[2 * i].start()
+
+    def relay(i):
+        @pl.when(zc == 0)
+        def _():
+            arrived(mid.at[i], mid_sem.at[i])
+            hops[2 * i + 1].start()
 
     arrived(sibq, sibw_sem.at[1])
     for k in range(2):
@@ -189,8 +213,8 @@
     xl, xr, xo = lax.rem(x + 3, 4), lax.rem(x + 1, 4), lax.rem(x + 2, 4)
 
     first_x = len(pending)
-    rights = [post(wpart(i, 2 * x, 2), xp.at[i], right, first_x + i) for i in range(5)]
-    lefts = [post(wpart(i, 2 * x, 2), xm.at[i], left, first_x + 5 + i) for i in range(5)]
+    rights = [post(wpart(i, 2 * x, 2), xp.at[i], right, first_x + i) for i in range(4)]
+    lefts = [post(wpart(i, 2 * x, 2), xm.at[i], left, first_x + 4 + i) for i in range(4)]
     pending.extend((None, copy) for copy in rights + lefts)
 
     def x1_stage(i):
@@ -217,8 +241,8 @@
         arrived(wpart(i, 2 * xo + 1), xmm.at[i])
         n = jnp.where(c == 0, i, i - 1)
         whole = wall.at[near + i]
-        when = None if 0 < i < 4 else (c == 0 if i == 0 else c == 1)
-        n = jnp.clip(n, 0, 3)
+        when = None if 0 < i < 3 else (c == 0 if i == 0 else c == 1)
+        n = jnp.clip(n, 0, 2)
         send(whole, whole, ssib.at[n], sib, z, when)
 
     def qpart(k, nk, slot, n):
@@ -276,6 +300,9 @@
         part = iota((512, C), 0)
         chan = channel(part, part >> 7)
         pick_all[...] = one_hot((iota((512, C), 1) == chan) & ((part & 15) < 12))
+        to, at = iota((128, 384), 0), iota((128, 384), 1)
+        same = (to >> 4) == ((at & 127) >> 4)
+        widen[...] = one_hot(same & ((at & 15) >= 12) & ((to & 15) == 4 * (at >> 7) + (at & 15) - 12))
         packed = iota((C, 512), 1)
         unpack[...] = one_hot((iota((C, 512), 0) == 12 * (packed >> 4) + (packed & 15)) & ((packed & 15) < 12))
 
@@ -314,20 +341,28 @@
 
             lax.fori_loop(0, 8, step, 0)
 
-    def taps(ta):
+    def taps(ta, frames=(0, 1)):
         t, a = ta // 3, lax.rem(ta, 3)
-        for j in range(2):
+        for j in frames:
             rows = pl.ds(pl.multiple_of(32 * a, 32), 256)
             acc[j] += dot_nt(act[j + t, rows, :], wall[ta])
 
     def own_taps(i):
         x3_stage(i)
         taps(near + i)
+
+    def spread(e):
+        units = wall[pl.ds(3 * e, 3)].reshape(384, 3 * C)
+        wall[7 + e] = dot_nn(widen[...], units).astype(BF)
 
     q_stage(0)
     constants()
     arrived(gain1, gain_sem.at[0])
     arrived(gain2, gain_sem.at[1])
+    relay(0)
+    relay(1)
+    relay(2)
+    relay(3)
     x1_stage(0)
     x1_stage(1)
     q_stage(1)
@@ -336,7 +371,6 @@
     x1_stage(3)
     x2_stage(1)
     q_stage(2)
-    x1_stage(4)
     x2_stage(2)
     arrived(mine, lat_sem.at[1])
     send(mine, halo, lat_sem.at[0], sib, z, c == 0)
@@ -347,28 +381,33 @@
     q_stage(3)
     arrived(halo, lat_sem.at[0])
     activate(0)
-    x2_stage(4)
     own_taps(0)
     own_taps(1)
-    q_stage(4)
     own_taps(2)
     own_taps(3)
-    own_taps(4)
-
-    def sib_taps(n, carry):
-        ta = jnp.where(c == 0, 5 + n, n)
-        arrived(wall.at[ta], ssib.at[n])
-        taps(ta)
-        return carry
-
-    lax.fori_loop(0, 4, sib_taps, 0)
+    spread(c)
+    taps(7 + c)
+
+    def sib_unit(n):
+        return jnp.where(c == 0, 4 + n, n)
+
+    for n in range(3):
+        arrived(wall.at[sib_unit(n)], ssib.at[n])
+    spread(1 - c)
+
     for j in range(2):
+
+        def sib_taps(n, carry):
+            taps(jnp.where(n == 3, 8 - c, sib_unit(n)), (j,))
+            return carry
+
+        lax.fori_loop(0, 4, sib_taps, 0)
         thr_s[j] = acc[j].astype(BF)
-
-    for k in range(4):
-        j = k % 2
-        dst = thr.at[:, pl.ds(pl.multiple_of(128 * zc, 128), 128)]
-        send_or_keep(thr_s.at[j], dst, exsem.at[zc], tm, 4 * g + k)
+        for k in (j, j + 2):
+            dst = thr.at[:, pl.ds(pl.multiple_of(128 * zc, 128), 128)]
+            send_or_keep(thr_s.at[j], dst, exsem.at[zc], tm, 4 * g + k)
+
+    q_stage(4)
     arrived(wq.at[pl.ds(2 * (1 - c), 2)], qsib)
     w_value = dot_nn(unpack[...], wq[2]).astype(BF)
     w_out = dot_nn(unpack[...], wq[3]).astype(BF)
@@ -410,7 +449,7 @@
 
 def body(latents, gain_one, conv_weight, gain_two, qkv_weight, out_weight):
     c = lax.rem(lax.axis_index("tm"), 2)
-    taps = conv_weight.reshape(9, 3, C, 6).transpose(0, 3, 1, 2).reshape(9, 6, 3 * C)
+    taps = jnp.pad(conv_weight.transpose(2, 0, 1), ((0, 0), (0, 5), (0, 0)))
     proj = jnp.concatenate([qkv_weight.transpose(0, 2, 1), out_weight.T[None]], 0)
 
     def placed(w):
@@ -428,9 +467,11 @@
         out_specs=vmem,
         scratch_shapes=[
             pltpu.VMEM((4, 8, 32, C), BF),
-            pltpu.VMEM((5, 16, 3 * C), BF),
+            pltpu.VMEM((7, 16, 3 * C), BF),
+            pltpu.VMEM((4, 16, 3 * C), BF),
             pltpu.VMEM((2, 16, C), BF),
-            pltpu.VMEM((5, 16, 3 * C), BF),
+            pltpu.VMEM((4, 16, 3 * C), BF),
+            pltpu.VMEM((4, 16, 3 * C), BF),
             pltpu.VMEM((9, 128, 3 * C), BF),
             pltpu.VMEM((4, 512, C), BF),
             pltpu.VMEM((4, 320, 3 * C), BF),
@@ -443,16 +484,17 @@
             pltpu.VMEM((C, 128), BF),
             pltpu.VMEM((512, C), BF),
             pltpu.VMEM((C, 512), BF),
+            pltpu.VMEM((128, 384), BF),
             pltpu.VMEM((C,), F32),
             pltpu.VMEM((C,), F32),
             dma((NSEND,)), dma((2,)), dma((2,)), dma((5,)), dma((5,)), dma((5,)), dma((5,)), dma((5,)), dma((5,)),
-            dma((4,)), dma((4,)), dma((8,)), dma, dma((4,)), dma((4,)), dma((2,)),
+            dma((4,)), dma((4,)), dma((8,)), dma, dma((4,)), dma((4,)), dma((2,)), dma((5,)),
         ],
         compiler_params=pltpu.CompilerParams(
             collective_id=0, has_side_effects=True, vmem_limit_bytes=40 * 1024 * 1024
         ),
         cost_estimate=pl.CostEstimate(flops=2 * 10**9, bytes_accessed=10**7, transcendentals=10**6),
-    )(latents[:, 0], placed(taps), placed(proj), gain_one, gain_two)
+    )(latents[:, 0], taps, placed(proj), gain_one, gain_two)
     return out[:, None]
 
 

time: 67.3 us -> 65 us (0.966)
  the two profiles are of different devices: /device:TPU:1 before, /device:TPU:2 now
where the time goes in v4:
time: 65 us; the launch traced here: 64.8 us
  Pallas kernels  62.3 us (96%)
  local copies, waits for them, and re-layouts  1.66 us (3%)
  other arithmetic  0.81 us (1%)
    pallas_call x1, Pallas kernels, body(): pl.pallas_call(kernel, out_shape=jax.ShapeDtypeStruct((4, 32, C), BF), in...  62.3 us
    unnamed x9, local copies, waits for them, and re-layouts  1.64 us

profile of v4, /device:TPU:2, one launch (start us, length us, event | category | flops | bytes accessed | tf_op | source)
XLA Modules:
  0.0 64.8 jit_solution(9411595822495284852)
XLA Ops:
  0.0 0.0 copy-start.3
  0.0 0.8 %pad_maximum_fusion = bf16[4,6,384]{2,1,0:T(8,128)(2,1)S(1)} fusion(bf16[1,6,384]{2,1,0:T(8,128)(2,1)} %bitcast.13, bf16[3,6,384]{2,1,0:T(8,128)(2,1)} %bitcast.12), kind=kLoop, calls=%fused_computation.1 | loop fusion | flops 9216 | bytes 36864 | tf_op jit(solution)/shard_map/concatenate | solution.py:453
  0.8 0.1 copy-done.3
  0.9 0.0 copy-start
  0.9 0.0 copy-start.1
  0.9 0.0 copy-start.2
  1.0 0.9 %copy-done = bf16[4,1,32,384]{3,2,1,0:T(8,128)(2,1)S(1)} copy-done((bf16[4,1,32,384]{3,2,1,0:T(8,128)(2,1)S(1)}, bf16[4,1,32,384]{3,2,1,0:T(8,128)(2,1)}, u32[]{:S(2)}) %copy-start) | copy-done | bytes 98328
  1.8 0.0 copy-done.1
  1.8 0.0 copy-done.2
  1.8 62.3 %shard_map.64 = bf16[4,32,384]{2,1,0:T(8,128)(2,1)S(1)} custom-call(bf16[4,32,384]{2,1,0:T(8,128)(2,1)S(1)} %bitcast.10, bf16[6,32,384]{2,1,0:T(8,128)(2,1)S(1)} %pad.12.wc_in, bf16[4,16,384]{2,1,0:T(8,128)(2,1)S(1)} %pad_select_fusion.wq_in, f32[384]{0:T(512)S(1)} %copy-done.1, f32[384]{0:T(512)S(1)} %copy-done.2), custom_call_target="tpu_custom_call" | custom-call | flops 2000000000 | bytes 10000000 | tf_op jit(solution)/shard_map/pallas_call | solution.py:463
  64.2 0.6 copy.9
  (2 shorter events, 0.0 us)
Async XLA Ops:
  0.0 0.9 %copy-start.3 = (bf16[27,384,6]{1,0,2:T(8,128)(2,1)S(1)}, bf16[27,384,6]{1,0,2:T(8,128)(2,1)}, u32[]{:S(2)}) copy-start(bf16[27,384,6]{1,0,2:T(8,128)(2,1)} %param.8) | copy-start | bytes 373252
  0.9 0.9 %copy-start = (bf16[4,1,32,384]{3,2,1,0:T(8,128)(2,1)S(1)}, bf16[4,1,32,384]{3,2,1,0:T(8,128)(2,1)}, u32[]{:S(2)}) copy-start(bf16[4,1,32,384]{3,2,1,0:T(8,128)(2,1)} %param.6) | copy-start | bytes 294916
  0.9 0.9 %copy-start.1 = (f32[384]{0:T(512)S(1)}, f32[384]{0:T(512)}, u32[]{:S(2)}) copy-start(f32[384]{0:T(512)} %gain1_in.1) | copy-start | bytes 4612
  0.9 0.9 %copy-start.2 = (f32[384]{0:T(512)S(1)}, f32[384]{0:T(512)}, u32[]{:S(2)}) copy-start(f32[384]{0:T(512)} %gain2_in.1) | copy-start | bytes 4612

commit v5 on v4

--- a/solution.py
+++ b/solution.py
@@ -52,7 +52,7 @@
 
 def kernel(
     lat_in, wc_in, wq_in, gain1_in, gain2_in, out_ref,
-    lat, wc, sibc, sibq, own, mid, wall, wq, act, acc, thr_s, thr, thrn, obuf, gmat, pick, pick_all, unpack, widen, gain1, gain2,
+    lat, wc, sibc, sibq, own, mid, wall, qpad, wq, act, acc, thr_s, thr, thrn, obuf, gmat, pick, pick_all, widen, gain1, gain2,
     sends, lat_sem, sibw_sem, yp, ym, xp, xm, xpp, xmm, ssib, qx, qy, qsib, exsem, outsem, gain_sem, mid_sem,
 ):
     tm = lax.axis_index("tm")
@@ -208,7 +208,7 @@
 
     arrived(sibq, sibw_sem.at[1])
     for k in range(2):
-        wq[2 * c + k, rows_of(q), :] = wq_in[2 * c + k] + sibq[k]
+        qpad[k, rows_of(x), :] = wq_in[2 * c + k] + sibq[k]
 
     xl, xr, xo = lax.rem(x + 3, 4), lax.rem(x + 1, 4), lax.rem(x + 2, 4)
 
@@ -245,41 +245,44 @@
         n = jnp.clip(n, 0, 2)
         send(whole, whole, ssib.at[n], sib, z, when)
 
-    def qpart(k, nk, slot, n):
-        return wq.at[pl.ds(2 * c + k, nk), rows_of(slot, n), :]
-
-    row = 4 * y
-
-    def q_row(step):
-        return 4 * lax.rem(y + 8 + step, 8)
+    def xpart(k, nk, xx):
+        return qpad.at[pl.ds(k, nk), rows_of(xx), :]
+
+    def ypart(k, nk, step):
+        yy = lax.rem(y + 8 + step, 8)
+        return wq.at[pl.ds(2 * c + k, nk), pl.ds(pl.multiple_of(48 * yy, 16), 48), :]
 
     def q_stage(s):
         if s == 0:
-            own = qpart(0, 2, q, 1)
-            send(own, own, qx.at[0], right, z)
-            send(own, own, qx.at[1], left, z)
+            piece = xpart(0, 2, x)
+            send(piece, piece, qx.at[0], right, z)
+            send(piece, piece, qx.at[1], left, z)
         elif s == 1:
-            arrived(qpart(0, 2, row + xl, 1), qx.at[0])
-            part = qpart(0, 1, row + xl, 1)
+            arrived(xpart(0, 2, xl), qx.at[0])
+            part = xpart(0, 1, xl)
             send(part, part, qx.at[2], right, z)
-            arrived(qpart(0, 2, row + xr, 1), qx.at[1])
-            part = qpart(1, 1, row + xr, 1)
+            arrived(xpart(0, 2, xr), qx.at[1])
+            part = xpart(1, 1, xr)
             send(part, part, qx.at[3], left, z)
         elif s == 2:
-            arrived(qpart(0, 1, row + xo, 1), qx.at[2])
-            arrived(qpart(1, 1, row + xo, 1), qx.at[3])
-            block = qpart(0, 2, row, 4)
+            arrived(xpart(0, 1, xo), qx.at[2])
+            arrived(xpart(1, 1, xo), qx.at[3])
+            wide = iota((48, 64), 0)
+            tight = one_hot(iota((48, 64), 1) == wide + 4 * twelfth(wide))
+            for k in range(2):
+                wq[2 * c + k, pl.ds(pl.multiple_of(48 * y, 16), 48), :] = dot_nn(tight, qpad[k]).astype(BF)
+            block = ypart(0, 2, 0)
             for n in range(4):
                 send(block, block, qy.at[n], near_y[n], z)
         elif s == 3:
             for n, step in enumerate((-1, 1, -2, 2)):
-                arrived(qpart(0, 2, q_row(step), 4), qy.at[n])
+                arrived(ypart(0, 2, step), qy.at[n])
             for n, (step, k, nk) in enumerate(((-1, 0, 2), (1, 0, 2), (-2, 0, 1), (2, 1, 1))):
-                block = qpart(k, nk, q_row(step), 4)
+                block = ypart(k, nk, step)
                 send(block, block, qy.at[4 + n], near_y[2 + n % 2], z)
         else:
             for n, (step, k, nk) in enumerate(((-3, 0, 2), (3, 0, 2), (4, 0, 1), (4, 1, 1))):
-                arrived(qpart(k, nk, q_row(step), 4), qy.at[4 + n])
+                arrived(ypart(k, nk, step), qy.at[4 + n])
             both = wq.at[kinds]
             send(both, both, qsib, sib, z)
 
@@ -303,8 +306,6 @@
         to, at = iota((128, 384), 0), iota((128, 384), 1)
         same = (to >> 4) == ((at & 127) >> 4)
         widen[...] = one_hot(same & ((at & 15) >= 12) & ((to & 15) == 4 * (at >> 7) + (at & 15) - 12))
-        packed = iota((C, 512), 1)
-        unpack[...] = one_hot((iota((C, 512), 0) == 12 * (packed >> 4) + (packed & 15)) & ((packed & 15) < 12))
 
     mine, halo = lat.at[pl.ds(2, 2)], lat.at[pl.ds(0, 2)]
 
@@ -369,8 +370,8 @@
     x1_stage(2)
     x2_stage(0)
     x1_stage(3)
+    q_stage(2)
     x2_stage(1)
-    q_stage(2)
     x2_stage(2)
     arrived(mine, lat_sem.at[1])
     send(mine, halo, lat_sem.at[0], sib, z, c == 0)
@@ -378,10 +379,10 @@
         acc[j] = dot_nn(lat[2 + j].reshape(256, C), pick[...])
     activate(1)
     x2_stage(3)
-    q_stage(3)
     arrived(halo, lat_sem.at[0])
     activate(0)
     own_taps(0)
+    q_stage(3)
     own_taps(1)
     own_taps(2)
     own_taps(3)
@@ -408,9 +409,6 @@
             send_or_keep(thr_s.at[j], dst, exsem.at[zc], tm, 4 * g + k)
 
     q_stage(4)
-    arrived(wq.at[pl.ds(2 * (1 - c), 2)], qsib)
-    w_value = dot_nn(unpack[...], wq[2]).astype(BF)
-    w_out = dot_nn(unpack[...], wq[3]).astype(BF)
     for k in range(4):
         arrived(thr.at[:, pl.ds(128 * k, 128)], exsem.at[k])
 
@@ -423,15 +421,16 @@
     normed = (dev * lax.rsqrt(var + 1e-06) * gain2[...].reshape(1, C)).astype(BF)
     thr[:, 0:C] = normed
 
+    arrived(wq.at[pl.ds(2 * (1 - c), 2)], qsib)
     mine_rows = pl.ds(pl.multiple_of(128 * half, 128), 128)
     queries = dot_nt(thr[mine_rows, 0:C], wq[0]).astype(BF)
     keys = dot_nt(normed, wq[1]).astype(BF)
-    values = dot_nt(normed, w_value).astype(BF)
+    values = dot_nt(normed, wq[2]).astype(BF)
     scores = dot_nt(queries, keys) * (C ** -0.5)
     expon = jnp.exp(scores - jnp.max(scores, axis=1, keepdims=True))
     totals = jnp.sum(expon, axis=1, keepdims=True)
     attended = (dot_nn(expon.astype(BF), values) / totals).astype(BF)
-    result = thrn[mine_rows, :] + dot_nt(attended, w_out)
+    result = thrn[mine_rows, :] + dot_nt(attended, wq[3])
     obuf[...] = result.astype(BF).reshape(4, 32, C)
 
     fr = 2 * c + fsel
@@ -473,7 +472,8 @@
             pltpu.VMEM((4, 16, 3 * C), BF),
             pltpu.VMEM((4, 16, 3 * C), BF),
             pltpu.VMEM((9, 128, 3 * C), BF),
-            pltpu.VMEM((4, 512, C), BF),
+            pltpu.VMEM((2, 64, C), BF),
+            pltpu.VMEM((4, C, C), BF),
             pltpu.VMEM((4, 320, 3 * C), BF),
             pltpu.VMEM((2, 256, 128), F32),
             pltpu.VMEM((2, 256, 128), BF),
@@ -483,7 +483,6 @@
             pltpu.VMEM((C, C), BF),
             pltpu.VMEM((C, 128), BF),
             pltpu.VMEM((512, C), BF),
-            pltpu.VMEM((C, 512), BF),
             pltpu.VMEM((128, 384), BF),
             pltpu.VMEM((C,), F32),
             pltpu.VMEM((C,), F32),

time: 65 us -> 57.8 us (0.89)
  the two profiles are of different devices: /device:TPU:2 before, /device:TPU:1 now
where the time goes in v5:
time: 57.8 us; the launch traced here: 57.6 us
  Pallas kernels  55.1 us (95%)
  local copies, waits for them, and re-layouts  1.66 us (3%)
  other arithmetic  0.81 us (1%)
    pallas_call x1, Pallas kernels, body(): pl.pallas_call(kernel, out_shape=jax.ShapeDtypeStruct((4, 32, C), BF), in...  55.1 us
    unnamed x9, local copies, waits for them, and re-layouts  1.64 us

profile of v5, /device:TPU:1, one launch (start us, length us, event | category | flops | bytes accessed | tf_op | source)
XLA Modules:
  0.0 57.6 jit_solution(16635558853598844336)
XLA Ops:
  0.0 0.0 copy-start.3
  0.0 0.8 %pad_maximum_fusion = bf16[4,6,384]{2,1,0:T(8,128)(2,1)S(1)} fusion(bf16[1,6,384]{2,1,0:T(8,128)(2,1)} %bitcast.13, bf16[3,6,384]{2,1,0:T(8,128)(2,1)} %bitcast.12), kind=kLoop, calls=%fused_computation.1 | loop fusion | flops 9216 | bytes 36864 | tf_op jit(solution)/shard_map/concatenate | solution.py:452
  0.8 0.1 copy-done.3
  0.9 0.0 copy-start
  0.9 0.0 copy-start.1
  0.9 0.0 copy-start.2
  1.0 0.9 %copy-done = bf16[4,1,32,384]{3,2,1,0:T(8,128)(2,1)S(1)} copy-done((bf16[4,1,32,384]{3,2,1,0:T(8,128)(2,1)S(1)}, bf16[4,1,32,384]{3,2,1,0:T(8,128)(2,1)}, u32[]{:S(2)}) %copy-start) | copy-done | bytes 98328
  1.8 0.0 copy-done.1
  1.8 0.0 copy-done.2
  1.8 55.1 %shard_map.64 = bf16[4,32,384]{2,1,0:T(8,128)(2,1)S(1)} custom-call(bf16[4,32,384]{2,1,0:T(8,128)(2,1)S(1)} %bitcast.10, bf16[6,32,384]{2,1,0:T(8,128)(2,1)S(1)} %pad.12.wc_in, bf16[4,16,384]{2,1,0:T(8,128)(2,1)S(1)} %pad_select_fusion.wq_in, f32[384]{0:T(512)S(1)} %copy-done.1, f32[384]{0:T(512)S(1)} %copy-done.2), custom_call_target="tpu_custom_call" | custom-call | flops 2000000000 | bytes 10000000 | tf_op jit(solution)/shard_map/pallas_call | solution.py:462
  56.9 0.6 %copy.9 = bf16[4,1,32,384]{3,2,1,0:T(8,128)(2,1)} copy(bf16[4,1,32,384]{3,2,1,0:T(8,128)(2,1)S(1)} %bitcast.9) | data formatting | bytes 196608
  (2 shorter events, 0.0 us)
Async XLA Ops:
  0.0 0.9 %copy-start.3 = (bf16[27,384,6]{1,0,2:T(8,128)(2,1)S(1)}, bf16[27,384,6]{1,0,2:T(8,128)(2,1)}, u32[]{:S(2)}) copy-start(bf16[27,384,6]{1,0,2:T(8,128)(2,1)} %param.8) | copy-start | bytes 373252
  0.9 0.9 %copy-start = (bf16[4,1,32,384]{3,2,1,0:T(8,128)(2,1)S(1)}, bf16[4,1,32,384]{3,2,1,0:T(8,128)(2,1)}, u32[]{:S(2)}) copy-start(bf16[4,1,32,384]{3,2,1,0:T(8,128)(2,1)} %param.6) | copy-start | bytes 294916
  0.9 0.9 %copy-start.1 = (f32[384]{0:T(512)S(1)}, f32[384]{0:T(512)}, u32[]{:S(2)}) copy-start(f32[384]{0:T(512)} %gain1_in.1) | copy-start | bytes 4612
  0.9 0.9 %copy-start.2 = (f32[384]{0:T(512)S(1)}, f32[384]{0:T(512)}, u32[]{:S(2)}) copy-start(f32[384]{0:T(512)} %gain2_in.1) | copy-start | bytes 4612

commit v6 on v5

--- a/solution.py
+++ b/solution.py
@@ -150,14 +150,9 @@
     far_row = jnp.where(zc == 0, 4, -zc)
 
     near, far = 3 * c, 3 * (1 - c)
-    send(wc.at[pl.ds(far, 4)], sibc, sibw_sem.at[0], sib, z)
-    send(wq_in.at[pl.ds(2 * (1 - c), 2)], sibq, sibw_sem.at[1], sib, z)
-
-    q_halo = lax.rem(q + c, 32)
-    for k in range(4):
-        send_or_keep(lat_in.at[pl.ds(0, 2)], lat.at[pl.ds(2, 2), z], lat_sem.at[1], 2 * q, 4 * c + k)
-        send_or_keep(lat_in.at[pl.ds(2, 2)], lat.at[pl.ds(2, 2), z], lat_sem.at[1], 2 * q + 1, 4 * c + k)
-        send_or_keep(lat_in.at[pl.ds(2, 2)], lat.at[pl.ds(0, 2), z], lat_sem.at[0], 2 * q_halo, 4 * (1 - c) + k)
+    for i in range(4):
+        send(wc.at[far + i], sibc.at[i], sibw_sem.at[i], sib, z)
+    send(wq_in.at[pl.ds(2 * (1 - c), 2)], sibq, sibw_sem.at[4], sib, z)
 
     def rows_of(slot, n=1):
         return pl.ds(pl.multiple_of(16 * slot, 16), 16 * n)
@@ -174,8 +169,8 @@
         )
 
     to_first, to_second = place(y - zc, x, c), place(y - far_row, x, c)
-    arrived(sibc, sibw_sem.at[0])
     for i in range(4):
+        arrived(sibc.at[i], sibw_sem.at[i])
         own[i] = wc[near + i] + sibc[i]
         for h, (to, sem) in enumerate(((to_first, yp), (to_second, ym))):
             copy = pltpu.make_async_remote_copy(
@@ -200,13 +195,19 @@
         for i in range(4):
             hops[2 * i].start()
 
+    q_halo = lax.rem(q + c, 32)
+    for k in range(4):
+        send_or_keep(lat_in.at[pl.ds(0, 2)], lat.at[pl.ds(2, 2), z], lat_sem.at[1], 2 * q, 4 * c + k)
+        send_or_keep(lat_in.at[pl.ds(2, 2)], lat.at[pl.ds(2, 2), z], lat_sem.at[1], 2 * q + 1, 4 * c + k)
+        send_or_keep(lat_in.at[pl.ds(2, 2)], lat.at[pl.ds(0, 2), z], lat_sem.at[0], 2 * q_halo, 4 * (1 - c) + k)
+
     def relay(i):
         @pl.when(zc == 0)
         def _():
             arrived(mid.at[i], mid_sem.at[i])
             hops[2 * i + 1].start()
 
-    arrived(sibq, sibw_sem.at[1])
+    arrived(sibq, sibw_sem.at[4])
     for k in range(2):
         qpad[k, rows_of(x), :] = wq_in[2 * c + k] + sibq[k]
 
@@ -486,7 +487,7 @@
             pltpu.VMEM((128, 384), BF),
             pltpu.VMEM((C,), F32),
             pltpu.VMEM((C,), F32),
-            dma((NSEND,)), dma((2,)), dma((2,)), dma((5,)), dma((5,)), dma((5,)), dma((5,)), dma((5,)), dma((5,)),
+            dma((NSEND,)), dma((2,)), dma((5,)), dma((5,)), dma((5,)), dma((5,)), dma((5,)), dma((5,)), dma((5,)),
             dma((4,)), dma((4,)), dma((8,)), dma, dma((4,)), dma((4,)), dma((2,)), dma((5,)),
         ],
         compiler_params=pltpu.CompilerParams(

time: 57.8 us -> 57.6 us (level)
  no operation moved by 1% of the time
where the time goes in v6:
time: 57.6 us; the launch traced here: 57.4 us
  Pallas kernels  54.9 us (95%)
  local copies, waits for them, and re-layouts  1.66 us (3%)
  other arithmetic  0.81 us (1%)
    pallas_call x1, Pallas kernels, body(): pl.pallas_call(kernel, out_shape=jax.ShapeDtypeStruct((4, 32, C), BF), in...  54.9 us
    unnamed x9, local copies, waits for them, and re-layouts  1.64 us

profile of v6, /device:TPU:1, one launch (start us, length us, event | category | flops | bytes accessed | tf_op | source)
XLA Modules:
  0.0 57.4 jit_solution(3125043672478471923)
XLA Ops:
  0.0 0.0 copy-start.3
  0.0 0.8 %pad_maximum_fusion = bf16[4,6,384]{2,1,0:T(8,128)(2,1)S(1)} fusion(bf16[1,6,384]{2,1,0:T(8,128)(2,1)} %bitcast.13, bf16[3,6,384]{2,1,0:T(8,128)(2,1)} %bitcast.12), kind=kLoop, calls=%fused_computation.1 | loop fusion | flops 9216 | bytes 36864 | tf_op jit(solution)/shard_map/concatenate | solution.py:453
  0.8 0.1 copy-done.3
  0.9 0.0 copy-start
  0.9 0.0 copy-start.1
  0.9 0.0 copy-start.2
  1.0 0.9 %copy-done = bf16[4,1,32,384]{3,2,1,0:T(8,128)(2,1)S(1)} copy-done((bf16[4,1,32,384]{3,2,1,0:T(8,128)(2,1)S(1)}, bf16[4,1,32,384]{3,2,1,0:T(8,128)(2,1)}, u32[]{:S(2)}) %copy-start) | copy-done | bytes 98328
  1.8 0.0 copy-done.1
  1.8 0.0 copy-done.2
  1.8 54.9 %shard_map.64 = bf16[4,32,384]{2,1,0:T(8,128)(2,1)S(1)} custom-call(bf16[4,32,384]{2,1,0:T(8,128)(2,1)S(1)} %bitcast.10, bf16[6,32,384]{2,1,0:T(8,128)(2,1)S(1)} %pad.12.wc_in, bf16[4,16,384]{2,1,0:T(8,128)(2,1)S(1)} %pad_select_fusion.wq_in, f32[384]{0:T(512)S(1)} %copy-done.1, f32[384]{0:T(512)S(1)} %copy-done.2), custom_call_target="tpu_custom_call" | custom-call | flops 2000000000 | bytes 10000000 | tf_op jit(solution)/shard_map/pallas_call | solution.py:463
  56.8 0.6 %copy.9 = bf16[4,1,32,384]{3,2,1,0:T(8,128)(2,1)} copy(bf16[4,1,32,384]{3,2,1,0:T(8,128)(2,1)S(1)} %bitcast.9) | data formatting | bytes 196608
  (2 shorter events, 0.0 us)
Async XLA Ops:
  0.0 0.9 %copy-start.3 = (bf16[27,384,6]{1,0,2:T(8,128)(2,1)S(1)}, bf16[27,384,6]{1,0,2:T(8,128)(2,1)}, u32[]{:S(2)}) copy-start(bf16[27,384,6]{1,0,2:T(8,128)(2,1)} %param.8) | copy-start | bytes 373252
  0.9 0.9 %copy-start = (bf16[4,1,32,384]{3,2,1,0:T(8,128)(2,1)S(1)}, bf16[4,1,32,384]{3,2,1,0:T(8,128)(2,1)}, u32[]{:S(2)}) copy-start(bf16[4,1,32,384]{3,2,1,0:T(8,128)(2,1)} %param.6) | copy-start | bytes 294916
  0.9 0.9 %copy-start.1 = (f32[384]{0:T(512)S(1)}, f32[384]{0:T(512)}, u32[]{:S(2)}) copy-start(f32[384]{0:T(512)} %gain1_in.1) | copy-start | bytes 4612
  0.9 0.9 %copy-start.2 = (f32[384]{0:T(512)S(1)}, f32[384]{0:T(512)}, u32[]{:S(2)}) copy-start(f32[384]{0:T(512)} %gain2_in.1) | copy-start | bytes 4612

commit v7 on v5

--- a/solution.py
+++ b/solution.py
@@ -92,6 +92,13 @@
 
     for k, (src, dst) in enumerate(((gain1_in, gain1), (gain2_in, gain2))):
         pltpu.make_async_copy(src, dst, gain_sem.at[k]).start()
+
+    def sent(copies):
+        for when, desc in copies:
+            if when is None:
+                desc.wait_send()
+            else:
+                pl.when(when)(desc.wait_send)
 
     barrier = pltpu.get_barrier_semaphore()
 
@@ -396,6 +403,8 @@
         arrived(wall.at[sib_unit(n)], ssib.at[n])
     spread(1 - c)
 
+    early = len(pending)
+
     for j in range(2):
 
         def sib_taps(n, carry):
@@ -409,6 +418,7 @@
             send_or_keep(thr_s.at[j], dst, exsem.at[zc], tm, 4 * g + k)
 
     q_stage(4)
+    sent(pending[:early])
     for k in range(4):
         arrived(thr.at[:, pl.ds(128 * k, 128)], exsem.at[k])
 
@@ -439,11 +449,7 @@
     for k in range(4):
         arrived(out_ref.at[k], outsem.at[k])
 
-    for when, desc in pending:
-        if when is None:
-            desc.wait_send()
-        else:
-            pl.when(when)(desc.wait_send)
+    sent(pending[early:])
 
 
 def body(latents, gain_one, conv_weight, gain_two, qkv_weight, out_weight):

time: 57.8 us -> 57.7 us (level)
  no operation moved by 1% of the time
where the time goes in v7:
time: 57.7 us; the launch traced here: 57.5 us
  Pallas kernels  55 us (95%)
  local copies, waits for them, and re-layouts  1.66 us (3%)
  other arithmetic  0.81 us (1%)
    pallas_call x1, Pallas kernels, body(): pl.pallas_call(kernel, out_shape=jax.ShapeDtypeStruct((4, 32, C), BF), in...  55 us
    unnamed x9, local copies, waits for them, and re-layouts  1.64 us

profile of v7, /device:TPU:1, one launch (start us, length us, event | category | flops | bytes accessed | tf_op | source)
XLA Modules:
  0.0 57.5 jit_solution(6640905224418703409)
XLA Ops:
  0.0 0.0 copy-start.3
  0.0 0.8 %pad_maximum_fusion = bf16[4,6,384]{2,1,0:T(8,128)(2,1)S(1)} fusion(bf16[1,6,384]{2,1,0:T(8,128)(2,1)} %bitcast.13, bf16[3,6,384]{2,1,0:T(8,128)(2,1)} %bitcast.12), kind=kLoop, calls=%fused_computation.1 | loop fusion | flops 9216 | bytes 36864 | tf_op jit(solution)/shard_map/concatenate | solution.py:458
  0.8 0.1 copy-done.3
  0.9 0.0 copy-start
  0.9 0.0 copy-start.1
  0.9 0.0 copy-start.2
  1.0 0.9 %copy-done = bf16[4,1,32,384]{3,2,1,0:T(8,128)(2,1)S(1)} copy-done((bf16[4,1,32,384]{3,2,1,0:T(8,128)(2,1)S(1)}, bf16[4,1,32,384]{3,2,1,0:T(8,128)(2,1)}, u32[]{:S(2)}) %copy-start) | copy-done | bytes 98328
  1.8 0.0 copy-done.1
  1.8 0.0 copy-done.2
  1.8 55.0 %shard_map.64 = bf16[4,32,384]{2,1,0:T(8,128)(2,1)S(1)} custom-call(bf16[4,32,384]{2,1,0:T(8,128)(2,1)S(1)} %bitcast.10, bf16[6,32,384]{2,1,0:T(8,128)(2,1)S(1)} %pad.12.wc_in, bf16[4,16,384]{2,1,0:T(8,128)(2,1)S(1)} %pad_select_fusion.wq_in, f32[384]{0:T(512)S(1)} %copy-done.1, f32[384]{0:T(512)S(1)} %copy-done.2), custom_call_target="tpu_custom_call" | custom-call | flops 2000000000 | bytes 10000000 | tf_op jit(solution)/shard_map/pallas_call | solution.py:468
  56.8 0.6 %copy.9 = bf16[4,1,32,384]{3,2,1,0:T(8,128)(2,1)} copy(bf16[4,1,32,384]{3,2,1,0:T(8,128)(2,1)S(1)} %bitcast.9) | data formatting | bytes 196608
  (2 shorter events, 0.0 us)
Async XLA Ops:
  0.0 0.9 %copy-start.3 = (bf16[27,384,6]{1,0,2:T(8,128)(2,1)S(1)}, bf16[27,384,6]{1,0,2:T(8,128)(2,1)}, u32[]{:S(2)}) copy-start(bf16[27,384,6]{1,0,2:T(8,128)(2,1)} %param.8) | copy-start | bytes 373252
  0.9 0.9 %copy-start = (bf16[4,1,32,384]{3,2,1,0:T(8,128)(2,1)S(1)}, bf16[4,1,32,384]{3,2,1,0:T(8,128)(2,1)}, u32[]{:S(2)}) copy-start(bf16[4,1,32,384]{3,2,1,0:T(8,128)(2,1)} %param.6) | copy-start | bytes 294916
  0.9 0.9 %copy-start.1 = (f32[384]{0:T(512)S(1)}, f32[384]{0:T(512)}, u32[]{:S(2)}) copy-start(f32[384]{0:T(512)} %gain1_in.1) | copy-start | bytes 4612
  0.9 0.9 %copy-start.2 = (f32[384]{0:T(512)S(1)}, f32[384]{0:T(512)}, u32[]{:S(2)}) copy-start(f32[384]{0:T(512)} %gain2_in.1) | copy-start | bytes 4612
